TPU v7x, 128 devices: a whole 4x4x4 slice. The times are simulated.
128 devices in a mesh: seq: 32 (over y, z, core), head: 4 (over x).
Axes of the slice: x: 4, y: 4, z: 4, core: 2. Of those that a mesh axis runs over, the one named last changes fastest.
Arguments:
- qkv: bfloat16 [3, 32768, 768], P(None, ('seq', 'head')), may hold values from -24 to 24
- offsets: int32 [12], P('head'), may hold values from 0 to 63
Outputs:
- attention: bfloat16 [32768, 768], P('seq', 'head')
Inputs may be any that keep to these rules, and one draw needn't show every extreme that they name: head h selects, at a level of dilation r, the positions congruent to offsets[h] mod r.
All inputs are finite; a program needn't handle non-finite values.
Results may differ from a plain program's by a relative error of at most 0.0045.
Values may be sent and summed in bfloat16 or wider, within the bound.
A program may use at most 64 MiB of HBM per device.

v0:
```python
import jax
import jax.numpy as jnp
from jax import lax
from jax.sharding import PartitionSpec as P

LEVELS = 4
GROWTH = 4


def pick_head(field_rows, dilation, offset_value):
    row_count, feat_dim = field_rows.shape
    folded = field_rows.reshape(row_count // dilation, dilation * feat_dim)
    start = offset_value % dilation * feat_dim
    return lax.dynamic_slice_in_dim(folded, start, feat_dim, 1)


def pick_heads(fields, dilation, offsets):
    return jnp.stack(
        [pick_head(fields[index], dilation, offsets[index]) for index in range(fields.shape[0])],
        axis=0,
    )


def attend_single(queries, keys_all, values_all):
    head_count, qcount, feat_dim = queries.shape
    block_rows = min(qcount, 512)
    softmax_scale = feat_dim ** (-0.5)
    blocks = jnp.moveaxis(
        queries.reshape(head_count, qcount // block_rows, block_rows, feat_dim), 1, 0
    )

    def one_block(query_block):
        scores = (
            jnp.einsum("hqe,hke->hqk", query_block, keys_all, preferred_element_type=jnp.float32)
            * softmax_scale
        )
        top_score = jnp.max(scores, axis=2)
        weights = jnp.exp(scores - top_score[:, :, None])
        denominator = jnp.sum(weights, axis=2)
        rounded = weights.astype(jnp.bfloat16)
        numerator = jnp.einsum(
            "hqk,hke->hqe", rounded, values_all, preferred_element_type=jnp.float32
        )
        return (numerator, denominator, top_score)

    numerator, denominator, top_score = lax.map(one_block, blocks)
    numerator = jnp.moveaxis(numerator, 0, 1).reshape(head_count, qcount, feat_dim)
    denominator = jnp.moveaxis(denominator, 0, 1).reshape(head_count, qcount)
    top_score = jnp.moveaxis(top_score, 0, 1).reshape(head_count, qcount)
    return (numerator, denominator, top_score)


def merge_level(running, update, dilation, offsets):
    run_num, run_den, run_top = running
    new_num, new_den, new_top = ([], [], [])
    for index in range(run_num.shape[0]):
        row_count, feat_dim = run_num[index].shape
        offset_value = offsets[index] % dilation
        num_view = run_num[index].reshape(row_count // dilation, dilation * feat_dim)
        den_view = run_den[index].reshape(row_count // dilation, dilation)
        top_view = run_top[index].reshape(row_count // dilation, dilation)
        old_num = lax.dynamic_slice_in_dim(num_view, offset_value * feat_dim, feat_dim, 1)
        old_den = lax.dynamic_slice_in_dim(den_view, offset_value, 1, 1)[:, 0]
        old_top = lax.dynamic_slice_in_dim(top_view, offset_value, 1, 1)[:, 0]
        both_top = jnp.maximum(old_top, update[2][index])
        old_factor = jnp.exp(old_top - both_top)
        new_factor = jnp.exp(update[2][index] - both_top)
        merged_num = old_num * old_factor[:, None] + update[0][index] * new_factor[:, None]
        merged_den = old_den * old_factor + update[1][index] * new_factor
        num_view = lax.dynamic_update_slice_in_dim(num_view, merged_num, offset_value * feat_dim, 1)
        den_view = lax.dynamic_update_slice_in_dim(den_view, merged_den[:, None], offset_value, 1)
        top_view = lax.dynamic_update_slice_in_dim(top_view, both_top[:, None], offset_value, 1)
        new_num.append(num_view.reshape(row_count, feat_dim))
        new_den.append(den_view.reshape(row_count))
        new_top.append(top_view.reshape(row_count))
    return (jnp.stack(new_num, 0), jnp.stack(new_den, 0), jnp.stack(new_top, 0))


def gather_partners(kv_tile, span_devices):
    position = lax.axis_index("seq")
    tile_rows = kv_tile.shape[1]
    whole_axis = lax.all_gather(kv_tile, "seq", axis=1, tiled=True)
    group_start = position // span_devices * (span_devices * tile_rows)
    collected = lax.dynamic_slice_in_dim(whole_axis, group_start, span_devices * tile_rows, 1)
    return collected


def per_device(qkv, offsets):
    local_rows = lax.all_to_all(qkv, "head", split_axis=2, concat_axis=1, tiled=True)
    tok_count = local_rows.shape[1]
    feat_cols = local_rows.shape[2]
    head_group = offsets.shape[0]
    head_dim = feat_cols // head_group
    seg_len = tok_count * lax.axis_size("seq") // GROWTH ** (LEVELS - 1)
    split_fields = local_rows.reshape(3, tok_count, head_group, head_dim)
    queries = jnp.moveaxis(split_fields[0], 1, 0)
    keys_all = jnp.moveaxis(split_fields[1], 1, 0)
    values_all = jnp.moveaxis(split_fields[2], 1, 0)
    running = None
    for level_index in range(LEVELS):
        dilation = GROWTH**level_index
        segment_len = seg_len * dilation
        picked_count = tok_count // dilation
        picked_queries = pick_heads(queries, dilation, offsets)
        picked_keys = pick_heads(keys_all, dilation, offsets)
        picked_values = pick_heads(values_all, dilation, offsets)
        if segment_len <= tok_count:
            groups = picked_count // seg_len
            shaped = tuple(
                (
                    jnp.moveaxis(field_rows.reshape(head_group, groups, seg_len, head_dim), 1, 0)
                    for field_rows in (picked_queries, picked_keys, picked_values)
                )
            )

            def per_group(triple):
                return attend_single(triple[0], triple[1], triple[2])

            numerator, denominator, top_score = lax.map(per_group, shaped)
            numerator = jnp.moveaxis(numerator, 0, 1).reshape(head_group, picked_count, head_dim)
            denominator = jnp.moveaxis(denominator, 0, 1).reshape(head_group, picked_count)
            top_score = jnp.moveaxis(top_score, 0, 1).reshape(head_group, picked_count)
        else:
            span_devices = segment_len // tok_count
            kv_tile = jnp.concatenate([picked_keys, picked_values], axis=2)
            collected = gather_partners(kv_tile, span_devices)
            segment_keys = collected[:, :, :head_dim]
            segment_values = collected[:, :, head_dim:]
            numerator, denominator, top_score = attend_single(
                picked_queries, segment_keys, segment_values
            )
        if level_index == 0:
            running = (numerator, denominator, top_score)
        else:
            running = merge_level(running, (numerator, denominator, top_score), dilation, offsets)
    result = running[0] / running[1][:, :, None]
    return jnp.concatenate([result[index] for index in range(head_group)], axis=1).astype(
        jnp.bfloat16
    )


def solution(mesh):
    return jax.shard_map(
        per_device,
        mesh=mesh,
        in_specs=(P(None, ("seq", "head"), None), P("head")),
        out_specs=P("seq", "head"),
        check_vma=False,
    )
```

profile of v0, /device:TPU:1, one launch (start us, length us, event | category | flops | bytes accessed | tf_op | source)
XLA Modules:
  0.0 173.6 jit_solution(456677064907921558)
XLA Ops:
  6.5 3.6 %copy.279 = bf16[3,256,768]{1,0,2:T(4,128)(2,1)} copy(bf16[3,256,768]{2,1,0:T(8,128)(2,1)} %param.4) | data formatting | bytes 2359296 | tf_op args[0]
  10.1 5.0 %all-to-all-start = ((bf16[3,256,768]{1,0,2:T(4,128)(2,1)}), bf16[3,256,768]{1,0,2:T(4,128)(2,1)S(1)}, u32[]{:S(2)}, u32[]{:S(2)}) async-start(bf16[3,256,768]{1,0,2:T(4,128)(2,1)} %copy.279), calls=%async_computation | async-start | bytes 3145728 | tf_op jit(solution)/shard_map/all_to_all | solution.py:89
  21.7 13.2 %all-to-all-done = bf16[3,256,768]{1,0,2:T(4,128)(2,1)S(1)} async-done(((bf16[3,256,768]{1,0,2:T(4,128)(2,1)}), bf16[3,256,768]{1,0,2:T(4,128)(2,1)S(1)}, u32[]{:S(2)}, u32[]{:S(2)}) %all-to-all-start) | async-done | bytes 1179680 | tf_op jit(solution)/shard_map/all_to_all | solution.py:89
  41.3 0.8 constant_dynamic-slice_fusion.31
  42.1 0.9 copy.307
  43.4 0.9 copy.301
  45.4 0.7 stack.156
  46.2 0.7 stack.155
  46.9 0.7 stack.154
  49.1 0.7 stack.152
  50.0 0.7 stack.151
  50.9 0.7 stack.150
  51.9 0.9 reshape_squeeze.112
  52.7 0.8 reshape_squeeze.121
  53.6 0.9 reshape_squeeze.111
  54.5 0.9 reshape_squeeze.120
  55.3 0.9 reshape_squeeze.110
  56.2 0.9 reshape_squeeze.119
  57.0 0.9 reshape_squeeze.133
  58.0 0.9 reshape_squeeze.136
  58.9 0.9 reshape_squeeze.132
  59.8 0.9 reshape_squeeze.135
  60.8 0.9 reshape_squeeze.131
  61.7 0.9 reshape_squeeze.134
  62.6 0.9 reshape_squeeze.130
  63.6 0.9 reshape_squeeze.128
  67.0 4.0 %while.14 = (s32[]{:T(128)}, f32[2,3,512,64]{2,3,1,0:T(8,128)S(1)}, f32[2,3,512]{2,1,0:T(4,128)S(1)}, f32[2,3,512]{2,1,0:T(4,128)S(1)}, bf16[2,3,512,64]{2,3,1,0...) while((s32[]{:T(128)}, f32[2,3,512,64]{2,3,1,0:T(8,128)S(1)}, ...), condition=%wide.region_3.4_spmd, body=%wide.region_0.3_spmd.sunk | while | flops 207614976 | bytes 10481761 | solution.py:119
  76.4 0.8 fusion.101
  77.1 0.8 fusion.100
  77.9 0.8 fusion.99
  78.8 27.9 %all_gather.11 = bf16[3,512,128]{2,1,0:T(8,128)(2,1)S(1)} all-gather(bf16[3,16,128]{2,1,0:T(8,128)(2,1)S(1)} %maximum_maximum_fusion.2), channel_id=1, replica_groups=mesh['seq'=32,'head'=4] {'seq'}, dimensions={1}, use_global_device_ids=true | all-gather | bytes 405504 | tf_op jit(solution)/shard_map/all_gather | solution.py:82
  106.7 0.7 fusion.98
  107.4 0.7 fusion.96
  112.1 0.8 dynamic-slice_bitcast_fusion.8
  112.9 0.8 dynamic-slice_bitcast_fusion.6
  113.7 0.9 fusion.28
  114.6 1.3 fusion.145
  116.0 0.8 fusion.34
  116.8 1.4 fusion.31
  118.2 23.5 %all-gather.3.cloned.1.call-done = bf16[3,8192,128]{1,2,0:T(8,128)(2,1)} async-done(((bf16[3,256,128]{1,2,0:T(8,128)(2,1)}), bf16[3,8192,128]{1,2,0:T(8,128)(2,1)}) %all-gather.3.cloned.1.call-update) | async-done | bytes 6291472 | tf_op jit(solution)/shard_map/all_gather | solution.py:82
  141.6 1.4 fusion.144
  145.1 0.8 copy.309
  146.7 0.8 copy.364
  151.8 1.4 fusion.25
  153.4 1.6 dynamic_update_slice.125
  155.2 1.1 dynamic_update_slice.115
  156.5 1.3 dynamic_update_slice.120
  165.8 0.9 copy.368
  (259 shorter events, 40.5 us)
Async XLA Ops:
  10.1 5.0 %copy-start.19 = (s32[3]{0:T(128)S(1)}, s32[3]{0:T(128)}, u32[]{:S(2)}) copy-start(s32[3]{0:T(128)} %param.5) | copy-start | bytes 40
  10.1 24.8 %all-to-all-start = ((bf16[3,256,768]{1,0,2:T(4,128)(2,1)}), bf16[3,256,768]{1,0,2:T(4,128)(2,1)S(1)}, u32[]{:S(2)}, u32[]{:S(2)}) async-start(bf16[3,256,768]{1,0,2:T(4,128)(2,1)} %copy.279), calls=%async_computation | async-start | bytes 3145728 | tf_op jit(solution)/shard_map/all_to_all | solution.py:89
  15.1 99.5 %all-gather.5.cloned.1.call-start = ((), (), s32[]{:S(2)}) async-start(), calls=%async_computation.2 | async-start | bytes 1622016 | tf_op jit(solution)/shard_map/all_gather | solution.py:82
  39.7 101.9 %all-gather.3.cloned.1.call-start = ((), (), s32[]{:S(2)}) async-start(), calls=%async_computation.1 | async-start | bytes 6488064 | tf_op jit(solution)/shard_map/all_gather | solution.py:82
  58.0 6.8 %copy-start.4 = (bf16[1,2,512,64]{2,1,3,0:T(2,128)(2,1)S(1)}, bf16[1,2,512,64]{2,1,3,0:T(2,128)(2,1)}, u32[]{:S(2)}) copy-start(bf16[1,2,512,64]{2,1,3,0:T(2,128)(2,1)} %stack.152) | copy-start | bytes 393220
  58.9 5.9 %copy-start.5 = (bf16[1,2,512,64]{2,1,3,0:T(2,128)(2,1)S(1)}, bf16[1,2,512,64]{2,1,3,0:T(2,128)(2,1)}, u32[]{:S(2)}) copy-start(bf16[1,2,512,64]{2,1,3,0:T(2,128)(2,1)} %stack.151) | copy-start | bytes 393220
  58.9 5.9 %copy-start.6 = (bf16[1,2,512,64]{2,1,3,0:T(2,128)(2,1)S(1)}, bf16[1,2,512,64]{2,1,3,0:T(2,128)(2,1)}, u32[]{:S(2)}) copy-start(bf16[1,2,512,64]{2,1,3,0:T(2,128)(2,1)} %stack.150) | copy-start | bytes 393220
  61.7 3.8 %copy-start = (bf16[1,2,512,64]{2,1,3,0:T(2,128)(2,1)S(1)}, bf16[1,2,512,64]{2,1,3,0:T(2,128)(2,1)}, u32[]{:S(2)}) copy-start(bf16[1,2,512,64]{2,1,3,0:T(2,128)(2,1)} %stack.156) | copy-start | bytes 393220
  61.7 3.8 %copy-start.2 = (bf16[1,2,512,64]{2,1,3,0:T(2,128)(2,1)S(1)}, bf16[1,2,512,64]{2,1,3,0:T(2,128)(2,1)}, u32[]{:S(2)}) copy-start(bf16[1,2,512,64]{2,1,3,0:T(2,128)(2,1)} %stack.155) | copy-start | bytes 393220
  61.7 3.8 %copy-start.3 = (bf16[1,2,512,64]{2,1,3,0:T(2,128)(2,1)S(1)}, bf16[1,2,512,64]{2,1,3,0:T(2,128)(2,1)}, u32[]{:S(2)}) copy-start(bf16[1,2,512,64]{2,1,3,0:T(2,128)(2,1)} %stack.154) | copy-start | bytes 393220
  64.8 1.5 copy-start.1
  65.5 1.4 copy-start.17
  71.0 0.9 copy-start.9
  71.0 1.1 copy-start.8
  71.0 1.3 copy-start.7
  144.8 3.5 %copy-start.28 = (f32[256,1]{0,1:T(1,128)S(1)}, f32[256,1]{0,1:T(1,128)}, u32[]{:S(2)}) copy-start(f32[256,1]{0,1:T(1,128)} %get-tuple-element.240) | copy-start | bytes 3076
  144.9 4.5 %copy-start.27 = (f32[256,1]{0,1:T(1,128)S(1)}, f32[256,1]{0,1:T(1,128)}, u32[]{:S(2)}) copy-start(f32[256,1]{0,1:T(1,128)} %get-tuple-element.241) | copy-start | bytes 3076
  144.9 5.6 %copy-start.26 = (f32[256,1]{0,1:T(1,128)S(1)}, f32[256,1]{0,1:T(1,128)}, u32[]{:S(2)}) copy-start(f32[256,1]{0,1:T(1,128)} %get-tuple-element.244) | copy-start | bytes 3076
  145.9 5.5 %copy-start.18 = (f32[3,64]{1,0:T(4,128)S(1)}, f32[3,64]{1,0:T(4,128)}, u32[]{:S(2)}) copy-start(f32[3,64]{1,0:T(4,128)} %fusion.34) | copy-start | bytes 2308
  150.1 3.1 %copy-start.10 = (f32[256,64]{0,1:T(8,128)S(1)}, f32[256,64]{0,1:T(8,128)}, u32[]{:S(2)}) copy-start(f32[256,64]{0,1:T(8,128)} %copy.378) | copy-start | bytes 196612
  150.1 3.1 %copy-start.20 = (f32[256,1]{0,1:T(1,128)S(1)}, f32[256,1]{0,1:T(1,128)}, u32[]{:S(2)}) copy-start(f32[256,1]{0,1:T(1,128)} %get-tuple-element.188) | copy-start | bytes 3076
  150.1 3.1 %copy-start.21 = (f32[256,1]{0,1:T(1,128)S(1)}, f32[256,1]{0,1:T(1,128)}, u32[]{:S(2)}) copy-start(f32[256,1]{0,1:T(1,128)} %get-tuple-element.189) | copy-start | bytes 3076
  150.2 3.1 %copy-start.22 = (f32[256,1]{0,1:T(1,128)S(1)}, f32[256,1]{0,1:T(1,128)}, u32[]{:S(2)}) copy-start(f32[256,1]{0,1:T(1,128)} %get-tuple-element.238) | copy-start | bytes 3076
  150.2 3.1 %copy-start.23 = (f32[256,1]{0,1:T(1,128)S(1)}, f32[256,1]{0,1:T(1,128)}, u32[]{:S(2)}) copy-start(f32[256,1]{0,1:T(1,128)} %get-tuple-element.239) | copy-start | bytes 3076
  150.2 3.1 %copy-start.24 = (f32[256,1]{0,1:T(1,128)S(1)}, f32[256,1]{0,1:T(1,128)}, u32[]{:S(2)}) copy-start(f32[256,1]{0,1:T(1,128)} %get-tuple-element.242) | copy-start | bytes 3076
  150.2 3.1 %copy-start.25 = (f32[256,1]{0,1:T(1,128)S(1)}, f32[256,1]{0,1:T(1,128)}, u32[]{:S(2)}) copy-start(f32[256,1]{0,1:T(1,128)} %get-tuple-element.243) | copy-start | bytes 3076
  157.8 4.2 %copy-start.16 = (f32[16,1]{1,0:T(8,128)S(1)}, f32[16,1]{1,0:T(8,128)}, u32[]{:S(2)}) copy-start(f32[16,1]{1,0:T(8,128)} %copy.357) | copy-start | bytes 196
  157.8 4.4 %copy-start.13 = (f32[16,1]{1,0:T(8,128)S(1)}, f32[16,1]{1,0:T(8,128)}, u32[]{:S(2)}) copy-start(f32[16,1]{1,0:T(8,128)} %copy.351) | copy-start | bytes 196
  157.8 4.4 %copy-start.15 = (f32[16,1]{1,0:T(8,128)S(1)}, f32[16,1]{1,0:T(8,128)}, u32[]{:S(2)}) copy-start(f32[16,1]{1,0:T(8,128)} %copy.367) | copy-start | bytes 196
  157.9 4.5 %copy-start.12 = (f32[16,1]{1,0:T(8,128)S(1)}, f32[16,1]{1,0:T(8,128)}, u32[]{:S(2)}) copy-start(f32[16,1]{1,0:T(8,128)} %copy.342) | copy-start | bytes 196
  157.9 4.5 %copy-start.14 = (f32[16,1]{1,0:T(8,128)S(1)}, f32[16,1]{1,0:T(8,128)}, u32[]{:S(2)}) copy-start(f32[16,1]{1,0:T(8,128)} %copy.362) | copy-start | bytes 196
  158.0 4.7 %copy-start.11 = (f32[3,16,64]{2,1,0:T(8,128)S(1)}, f32[3,16,64]{2,1,0:T(8,128)}, u32[]{:S(2)}) copy-start(f32[3,16,64]{2,1,0:T(8,128)} %fusion.28) | copy-start | bytes 36868
Sparse Core Ops, SparseCore 0:
  39.8 45.6 all-gather.4
  87.7 53.9 all-gather.2
where the time goes:
time: 174 us
  local copies, waits for them, and re-layouts  65 us (37%)
  waiting for transfers between devices  36.7 us (21%)
  blocking collectives  27.9 us (16%)
  between operations  20.8 us (12%)
  matrix products  9.35 us (5%)
  other arithmetic  8.34 us (5%)
  starting transfers between devices  5.2 us (3%)
    all_gather x1, blocking collectives, gather_partners(): whole_axis = lax.all_gather(kv_tile, 'seq', axis=1, tiled=True)  27.9 us
    all_gather x2, waiting for transfers between devices, gather_partners(): whole_axis = lax.all_gather(kv_tile, 'seq', axis=1, tiled=True)  23.5 us
    another operation x27, local copies, waits for them, and re-layouts, pick_head(): folded = field_rows.reshape(row_count // dilation, dilation * feat_dim)  15.4 us
    all_to_all x1, waiting for transfers between devices, per_device(): lax.all_to_all(qkv, 'head', split_axis=2, concat_axis=1, tiled=True)  13.2 us
    another operation x19, local copies, waits for them, and re-layouts, pick_heads(): jnp.stack([pick_head(fields[index], dilation, offsets[index]) for index i...  10.9 us
    dynamic_update_slice x9, local copies, waits for them, and re-layouts, merge_level(): lax.dynamic_update_slice_in_dim(num_view, merged_num, offset_value * feat...  6.54 us
    unnamed x74, local copies, waits for them, and re-layouts  5.92 us
    dot_general x5, matrix products, one_block(): jnp.einsum('hqk,hke->hqe', rounded, values_all, preferred_element_type=jn...  5.01 us
  transfers between devices with their start and end apart: 3, of which 2 were waited for; matrix products, arithmetic and copies ran while one was open for 29% of the time, Pallas kernels for 0%

commit v1 on v0

v1 whole, which is shorter than its diff:
```python
import jax
import jax.numpy as jnp
from jax import lax
from jax.experimental import pallas as pl
from jax.experimental.pallas import tpu as pltpu
from jax.sharding import PartitionSpec as P

HD = 64
GH = 3
NX = 4
NZ = 4
ROWS = 256
MESH = pl.DeviceIdType.MESH
LOW = -1.0e30
BF = jnp.bfloat16
F32 = jnp.float32

L2_STEPS = [(0, dz, dc) for dz in (1, 2, 3) for dc in (0, 1)]
L3_STEPS = [(dy, dz, dc) for dy in (1, 2, 3) for dz in range(NZ) for dc in (0, 1)]


def iota(shape, dim):
    return lax.broadcasted_iota(jnp.int32, shape, dim)


def dot(a, b):
    return jnp.dot(a, b, preferred_element_type=F32)


def dot_t(a, b):
    return lax.dot_general(a, b, (((1,), (1,)), ((), ())), preferred_element_type=F32)


def source_row(i):
    return (i % 4) * 64 + (i // 4 % 4) * 16 + (i // 16 % 4) * 4 + i // 64


def digits_of(o):
    return o & 3, (o >> 2) & 3, (o >> 4) & 3


def bits(o, shape):
    spread_out = jnp.zeros(shape, jnp.int32) + o
    return [(spread_out >> i) & 1 == 1 for i in range(4)]


def turn(parts, mask, step):
    return [jnp.where(mask, parts[(i + step) % len(parts)], part) for i, part in enumerate(parts)]


def pick(four, low_bit, high_bit):
    return jnp.where(high_bit, jnp.where(low_bit, four[3], four[2]), jnp.where(low_bit, four[1], four[0]))


def lanes_low(shape):
    return iota(shape, 1) < HD


def soften(scores):
    top = jnp.max(scores, axis=1, keepdims=True)
    return jnp.exp(scores - top).astype(BF), top


def ones_and_values(kv):
    return jnp.where(lanes_low(kv.shape), jnp.ones_like(kv), kv)


def merge(a, a_top, b, b_top):
    top = jnp.maximum(a_top, b_top)
    return a * jnp.exp(a_top - top) + b * jnp.exp(b_top - top), top


def spread(part, w):
    pieces = []
    for j in range(NX):
        pieces += [part[j * w : (j + 1) * w]] * 4
    return jnp.concatenate(pieces, axis=0)


def kernel(
    qkv, offs, out,
    xin, perm, qs, kvs, kvrel, qr, qz, kv, k1s, q2s, k2, k3own, k3, sm, n0, t0, n1, t1, outp,
    in_sem, own_sem, o_send, o_recv, q_send, q_recv, s_send, s_recv, r_send, r_recv,
    c_send, c_recv, l2_send, l2_recv, l3_send, l3_recv,
):
    s = lax.axis_index("seq")
    x = lax.axis_index("head")
    core, z, y = s % 2, s // 2 % NZ, s // (2 * NZ)

    def along_x(k):
        return (s, (x + k) % NX)

    def along_seq(step):
        dy, dz, dc = step
        return ((y + dy) % 4 * (2 * NZ) + (z + dz) % NZ * 2 + (core + dc) % 2, x)

    sibling = along_seq((0, 0, 1))
    barrier = pltpu.get_barrier_semaphore()
    peers = [along_x(k) for k in (1, 2, 3)] + [sibling] + [along_seq(t) for t in L2_STEPS + L3_STEPS]
    for peer in peers:
        pl.semaphore_signal(barrier, inc=1, device_id=peer, device_id_type=MESH)

    loads = [pltpu.make_async_copy(qkv.at[i], xin.at[i], in_sem.at[i]) for i in range(3)]
    for load in loads:
        load.start()

    def remote(src, dst, send, recv, peer):
        return pltpu.make_async_remote_copy(
            src_ref=src, dst_ref=dst, send_sem=send, recv_sem=recv, device_id=peer, device_id_type=MESH
        )

    a, b = iota((ROWS, ROWS), 0), iota((ROWS, ROWS), 1)
    forth = jnp.where(b == source_row(a), 1.0, 0.0).astype(BF)
    perm[...] = jnp.where(a == source_row(b), 1.0, 0.0).astype(BF)
    low = lanes_low((ROWS, 128))
    low_half = lanes_low((128, 128))

    for i in range(GH):
        sm[x, i] = offs[i]

    loads[0].wait()
    forth_scaled = forth * jnp.asarray(HD**-0.5, BF)
    for t in range(3):
        wide = dot(forth_scaled, xin[0, :, t * 256 : (t + 1) * 256])
        for u in range(4):
            head = 4 * t + u
            tile = wide[:, u // 2 * 128 : (u // 2 + 1) * 128]
            first, second = tile[:128], tile[128:]
            if u % 2 == 0:
                packed = jnp.where(low_half, first, pltpu.roll(second, HD, 1))
            else:
                packed = jnp.where(low_half, pltpu.roll(first, HD, 1), second)
            qs[head // GH, head % GH] = packed.astype(BF)

    pl.semaphore_wait(barrier, len(peers))
    sends = []

    def send(*args):
        copy = remote(*args)
        copy.start()
        sends.append(copy)
        return copy

    o_copies = [send(sm.at[x], sm.at[x], o_send.at[k - 1], o_recv.at[k - 1], along_x(k)) for k in (1, 2, 3)]
    q_copies = [
        [
            send(qs.at[(x + k) % NX, hh], qr.at[hh, x], q_send.at[hh, k - 1], q_recv.at[hh, k - 1], along_x(k))
            for k in (1, 3, 2)
        ]
        for hh in range(GH)
    ]
    own_q = pltpu.make_async_copy(qs.at[x], qr.at[:, x], own_sem.at[0])
    own_q.start()

    loads[1].wait()
    loads[2].wait()
    for t in range(6):
        both = jnp.concatenate(
            [xin[1, :, t * 128 : (t + 1) * 128], xin[2, :, t * 128 : (t + 1) * 128]], axis=1
        )
        wide = dot(forth, both)
        keys, values = wide[:, :128], wide[:, 128:]
        even = jnp.where(low, keys, pltpu.roll(values, HD, 1))
        odd = jnp.where(low, pltpu.roll(keys, HD, 1), values)
        for head, packed in ((2 * t, even), (2 * t + 1, odd)):
            kvs[head // GH, head % GH] = packed.astype(BF)

    for copy in o_copies:
        copy.wait_recv()
    for g in range(NX):
        for hh in range(GH):
            b0, b1, b2, b3 = bits(sm[g, hh], (16, 128))
            parts = [kvs[g, hh, i * 16 : (i + 1) * 16, :] for i in range(16)]
            parts = turn(turn(parts, b0, 4), b1, 8)
            parts[:4] = turn(turn(parts[:4], b2, 1), b3, 2)
            for i in range(16):
                kvrel[g, hh, i * 16 : (i + 1) * 16, :] = parts[i]
    s_copies = [
        send(
            kvrel.at[(x + k) % NX, :, pl.ds(0, 64), :], kv.at[:, x, pl.ds(0, 64), :],
            s_send.at[k - 1], s_recv.at[k - 1], along_x(k),
        )
        for k in (1, 3, 2)
    ]
    r_copies = [
        [
            send(
                kvrel.at[(x + k) % NX, hh, pl.ds(64, 192), :], kv.at[hh, x, pl.ds(64, 192), :],
                r_send.at[hh, k - 1], r_recv.at[hh, k - 1], along_x(k),
            )
            for k in (1, 3, 2)
        ]
        for hh in range(GH)
    ]
    own_kv = pltpu.make_async_copy(kvrel.at[x], kv.at[:, x], own_sem.at[1])
    own_kv.start()

    digits = []
    for hh in range(GH):
        o = sm[x, hh]
        digits.append(digits_of(o))

    own_q.wait()
    for hh in range(GH):
        for copy in q_copies[hh]:
            copy.wait_recv()
        for j in range(NX):
            tile = qr[hh, j].astype(F32)
            qz[hh, j, 0:128, :] = jnp.where(low_half, tile, 0.0).astype(BF)
            qz[hh, j, 128:256, :] = jnp.where(low_half, pltpu.roll(tile, HD, 1), 0.0).astype(BF)

    own_kv.wait()
    for copy in s_copies:
        copy.wait_recv()
    c_copy = send(kv.at[:, :, pl.ds(0, 64), :], k1s, c_send, c_recv, sibling)
    l2_copies = [
        send(kv.at[:, :, pl.ds(0, 16), :], k2.at[i], l2_send.at[i], l2_recv.at[i], along_seq(step))
        for i, step in enumerate(L2_STEPS)
    ]
    e_row, e_col = iota((16, 64), 0), iota((16, 64), 1)
    for hh in range(GH):
        chosen = jnp.where(e_col == e_row // 4 * 16 + digits[hh][2] * 4 + e_row % 4, 1.0, 0.0).astype(BF)
        k3own[hh] = dot(chosen, kv[hh, :, 0:16, :].reshape(64, 128)).astype(BF)
    l3_copies = [
        send(k3own, k3.at[i], l3_send.at[i], l3_recv.at[i], along_seq(step)) for i, step in enumerate(L3_STEPS)
    ]

    c_copy.wait_recv()
    for hh in range(GH):
        b0, b1, b2, b3 = bits(sm[x, hh], (16, 128))
        q1 = []
        for j in range(NX):
            parts = [qz[hh, j, i * 16 : (i + 1) * 16, :] for i in range(16)]
            chosen = [pick(parts[i::4], b0, b1) for i in range(4)]
            q1 += chosen
            q2s[hh, j] = pick(chosen, b2, b3)
        q1 = jnp.concatenate(q1, axis=0)
        keys = jnp.concatenate([kv[hh, :, 0:64, :].reshape(256, 128), k1s[hh].reshape(256, 128)], axis=0)
        weights, top = soften(dot_t(q1, keys))
        n1[hh] = dot(weights, ones_and_values(keys))
        t1[hh] = top

    for hh in range(GH):
        for copy in r_copies[hh]:
            copy.wait_recv()
        for seg in range(2):
            keys = kv[hh, 2 * seg : 2 * seg + 2].reshape(512, 128)
            values = ones_and_values(keys)
            for j in (2 * seg, 2 * seg + 1):
                weights, top = soften(dot_t(qz[hh, j], keys))
                n0[hh, j] = dot(weights, values)
                t0[hh, j] = top

    for copy in l2_copies + l3_copies:
        copy.wait_recv()
    col = iota((64, 512), 1)
    for hh in range(GH):
        c1, c2, c3 = digits[hh]
        q2 = q2s[hh].reshape(64, 128)
        keys2 = jnp.concatenate(
            [kv[hh, :, 0:16, :].reshape(64, 128), k1s[hh, :, 0:16, :].reshape(64, 128)]
            + [k2[i, hh].reshape(64, 128) for i in range(len(L2_STEPS))],
            axis=0,
        )
        keys3 = jnp.concatenate([k3[i, hh] for i in range(len(L3_STEPS))], axis=0)
        scores2 = dot_t(q2, keys2)
        scores3 = jnp.concatenate(
            [jnp.where(col % 16 // 4 == c3, scores2, LOW), dot_t(q2, keys3)], axis=1
        )
        weights2, top2 = soften(scores2)
        weights3, top3 = soften(scores3)
        values2 = ones_and_values(keys2)
        num2 = dot(weights2, values2)
        num3 = dot(weights3[:, :512], values2) + dot(weights3[:, 512:], ones_and_values(keys3))
        row = iota((64, 1), 0)
        num2, top2 = merge(num2, top2, num3, jnp.where(row % 16 // 4 == c3, top3, LOW))

        row = iota((ROWS, 1), 0)
        num1, top1 = merge(
            n1[hh], t1[hh], spread(num2, 16), jnp.where(row % 64 // 16 == c2, spread(top2, 16), LOW)
        )

        b0, b1, _, _ = bits(sm[x, hh], (64, 128))
        part = jnp.concatenate(
            [pick([n0[hh, j, i * 64 : (i + 1) * 64, :] for i in range(4)], b0, b1) for j in range(NX)], axis=0
        )
        b0, b1, _, _ = bits(sm[x, hh], (64, 1))
        part_top = jnp.concatenate(
            [pick([t0[hh, j, i * 64 : (i + 1) * 64, :] for i in range(4)], b0, b1) for j in range(NX)], axis=0
        )
        num0, _ = merge(part, part_top, num1, top1)
        low64 = lanes_low((64, 128))
        for j in range(NX):
            merged = num0[j * 64 : (j + 1) * 64]
            whole = n0[hh, j]
            mine = iota((ROWS, 1), 0) // 64 == c1
            whole = jnp.where(mine, jnp.concatenate([merged] * 4, axis=0), whole)
            turned = pltpu.roll(whole, HD, 1)
            if hh % 2 == 0:
                value = (turned / whole).astype(BF)
                outp[j, :, hh // 2 * 128 : (hh // 2 + 1) * 128] = value
            else:
                value = (whole / turned).astype(BF)
                outp[j, :, 0:128] = jnp.where(low, outp[j, :, 0:128], value)
    for j in range(NX):
        final = dot(perm[...], outp[j])
        out[j * ROWS : (j + 1) * ROWS, :] = final[:, : GH * HD].astype(BF)

    for copy in sends:
        copy.wait_send()


def per_device(qkv, offsets):
    dma = pltpu.SemaphoreType.DMA
    return pl.pallas_call(
        kernel,
        out_shape=jax.ShapeDtypeStruct((NX * ROWS, GH * HD), BF),
        in_specs=[pl.BlockSpec(memory_space=pl.ANY), pl.BlockSpec(memory_space=pltpu.SMEM)],
        out_specs=pl.BlockSpec(memory_space=pltpu.VMEM),
        scratch_shapes=[
            pltpu.VMEM((3, ROWS, 768), BF),
            pltpu.VMEM((ROWS, ROWS), BF),
            pltpu.VMEM((NX, GH, 128, 128), BF),
            pltpu.VMEM((NX, GH, ROWS, 128), BF),
            pltpu.VMEM((NX, GH, ROWS, 128), BF),
            pltpu.VMEM((GH, NX, 128, 128), BF),
            pltpu.VMEM((GH, NX, ROWS, 128), BF),
            pltpu.VMEM((GH, NX, ROWS, 128), BF),
            pltpu.VMEM((GH, NX, 64, 128), BF),
            pltpu.VMEM((GH, NX, 16, 128), BF),
            pltpu.VMEM((len(L2_STEPS), GH, NX, 16, 128), BF),
            pltpu.VMEM((GH, 16, 128), BF),
            pltpu.VMEM((len(L3_STEPS), GH, 16, 128), BF),
            pltpu.SMEM((NX, 128), jnp.int32),
            pltpu.VMEM((GH, NX, ROWS, 128), F32),
            pltpu.VMEM((GH, NX, ROWS, 1), F32),
            pltpu.VMEM((GH, ROWS, 128), F32),
            pltpu.VMEM((GH, ROWS, 1), F32),
            pltpu.VMEM((NX, ROWS, 256), BF),
            dma((3,)), dma((2,)), dma((3,)), dma((3,)),
            dma((GH, 3)), dma((GH, 3)), dma((3,)), dma((3,)), dma((GH, 3)), dma((GH, 3)),
            dma, dma, dma((len(L2_STEPS),)), dma((len(L2_STEPS),)), dma((len(L3_STEPS),)), dma((len(L3_STEPS),)),
        ],
        compiler_params=pltpu.CompilerParams(
            collective_id=0, has_side_effects=True, vmem_limit_bytes=40 * 2**20
        ),
        cost_estimate=pl.CostEstimate(flops=10**9, bytes_accessed=2 * 10**6, transcendentals=2 * 10**6),
    )(qkv, offsets)


def solution(mesh):
    return jax.shard_map(
        per_device,
        mesh=mesh,
        in_specs=(P(None, ("seq", "head"), None), P("head")),
        out_specs=P("seq", "head"),
        check_vma=False,
    )
```

time: 174 us -> 34 us (0.20)
  local copies, waits for them, and re-layouts: 65 us -> 2.86 us
  waiting for transfers between devices: 36.7 us -> 0 us
  Pallas kernels: 0 us -> 31 us
  blocking collectives: 27.9 us -> 0 us
  between operations: 20.8 us -> 0.01 us
  matrix products: 9.35 us -> 0 us
  other arithmetic: 8.34 us -> 0 us
  starting transfers between devices: 5.2 us -> 0 us
    pallas_call x0 -> x1, Pallas kernels: none -> 31 us  [per_device(): pl.pallas_call(kernel, out_shape=jax.ShapeDtypeStruct((NX * ROWS, GH * HD...]
    another operation x79 -> x0, local copies, waits for them, and re-layouts: 30.1 us -> none  [the longest x27 15.4 us: pick_head(): folded = field_rows.reshape(row_count // dilation, dilation * feat_dim)]
    all_gather x1 -> x0, blocking collectives: 27.9 us -> none  [gather_partners(): whole_axis = lax.all_gather(kv_tile, 'seq', axis=1, tiled=True)]
    all_gather x2 -> x0, waiting for transfers between devices: 23.5 us -> none  [gather_partners(): whole_axis = lax.all_gather(kv_tile, 'seq', axis=1, tiled=True)]
    all_to_all x1 -> x0, waiting for transfers between devices: 13.2 us -> none  [per_device(): lax.all_to_all(qkv, 'head', split_axis=2, concat_axis=1, tiled=True)]
    dynamic_update_slice x26 -> x0, local copies, waits for them, and re-layouts: 11.4 us -> none  [the longest x9 6.54 us: merge_level(): lax.dynamic_update_slice_in_dim(num_view, merged_num, offset_value * feat...]
    dot_general x10 -> x0, matrix products: 9.35 us -> none  [the longest x5 5.01 us: one_block(): jnp.einsum('hqk,hke->hqe', rounded, values_all, preferred_element_type=jn...]
    all_to_all x1 -> x0, starting transfers between devices: 4.97 us -> none  [per_device(): lax.all_to_all(qkv, 'head', split_axis=2, concat_axis=1, tiled=True)]
  transfers between devices with their start and end apart: 3 -> 0, of which waited for: 2 -> 0; matrix products, arithmetic and copies ran while one was open for 29% -> 0% of each run, Pallas kernels for 0% -> 0%
where the time goes in v1:
time: 34 us; the launch traced here: 33.9 us
  Pallas kernels  31 us (91%)
  local copies, waits for them, and re-layouts  2.86 us (8%)
    pallas_call x1, Pallas kernels, per_device(): pl.pallas_call(kernel, out_shape=jax.ShapeDtypeStruct((NX * ROWS, GH * HD...  31 us
    unnamed x4, local copies, waits for them, and re-layouts  1.92 us
    pallas_call x1, local copies, waits for them, and re-layouts, per_device(): pl.pallas_call(kernel, out_shape=jax.ShapeDtypeStruct((NX * ROWS, GH * HD...  0.94 us

profile of v1, /device:TPU:1, one launch (start us, length us, event | category | flops | bytes accessed | tf_op | source)
XLA Modules:
  0.0 33.9 jit_solution(8880001623320705191)
XLA Ops:
  0.0 0.0 copy-start
  0.0 1.3 %copy-done = bf16[3,256,768]{2,1,0:T(8,128)(2,1)S(1)} copy-done((bf16[3,256,768]{2,1,0:T(8,128)(2,1)S(1)}, bf16[3,256,768]{2,1,0:T(8,128)(2,1)}, u32[]{:S(2)}) %copy-start) | copy-done | bytes 1179672
  1.3 0.0 copy-start.1
  1.3 0.7 %copy-done.1 = s32[3]{0:T(128)S(1)} copy-done((s32[3]{0:T(128)S(1)}, s32[3]{0:T(128)}, u32[]{:S(2)}) %copy-start.1) | copy-done | bytes 36
  1.9 31.0 %shard_map.28 = bf16[1024,192]{1,0:T(8,128)(2,1)S(1)} custom-call(bf16[3,256,768]{2,1,0:T(8,128)(2,1)S(1)} %copy-done, s32[3]{0:T(128)S(1)} %copy-done.1), custom_call_target="tpu_custom_call" | custom-call | flops 1000000000 | bytes 2000000 | tf_op jit(solution)/shard_map/pallas_call | solution.py:315
  32.9 0.9 %copy.3 = bf16[1024,192]{0,1:T(8,128)(2,1)} copy(bf16[1024,192]{1,0:T(8,128)(2,1)S(1)} %shard_map.28) | data formatting | bytes 786432 | tf_op jit(solution)/shard_map/pallas_call | solution.py:315
Async XLA Ops:
  0.0 1.3 %copy-start = (bf16[3,256,768]{2,1,0:T(8,128)(2,1)S(1)}, bf16[3,256,768]{2,1,0:T(8,128)(2,1)}, u32[]{:S(2)}) copy-start(bf16[3,256,768]{2,1,0:T(8,128)(2,1)} %qkv.1) | copy-start | bytes 3538948
  1.3 0.7 %copy-start.1 = (s32[3]{0:T(128)S(1)}, s32[3]{0:T(128)}, u32[]{:S(2)}) copy-start(s32[3]{0:T(128)} %offs.1) | copy-start | bytes 40

commit v2 on v1

v2 whole, which is shorter than its diff:
```python
import jax
import jax.numpy as jnp
from jax import lax
from jax.experimental import pallas as pl
from jax.experimental.pallas import tpu as pltpu
from jax.sharding import PartitionSpec as P

HD = 64
GH = 3
NX = 4
NY = 4
NZ = 4
ROWS = 256
MESH = pl.DeviceIdType.MESH
LOW = -1.0e30
BF = jnp.bfloat16
F32 = jnp.float32

L2_STEPS = [(0, dz) for dz in (2, 1, 3)]
L3_STEPS = [(dy, dz) for dy in (2, 1, 3) for dz in (2, 1, 3, 0)]
N2, N3 = len(L2_STEPS), len(L3_STEPS)


def iota(shape, dim):
    return lax.broadcasted_iota(jnp.int32, shape, dim)


def dot(a, b):
    return jnp.dot(a, b, preferred_element_type=F32)


def dot_t(a, b):
    return lax.dot_general(a, b, (((1,), (1,)), ((), ())), preferred_element_type=F32)


def source_row(i):
    return (i % 4) * 64 + (i // 4 % 4) * 16 + (i // 16 % 4) * 4 + i // 64


def bits(o, shape):
    spread_out = jnp.zeros(shape, jnp.int32) + o
    return [(spread_out >> i) & 1 == 1 for i in range(4)]


def turn(parts, mask, step):
    return [jnp.where(mask, parts[(i + step) % len(parts)], part) for i, part in enumerate(parts)]


def pick(four, low_bit, high_bit):
    return jnp.where(high_bit, jnp.where(low_bit, four[3], four[2]), jnp.where(low_bit, four[1], four[0]))


def lanes_low(shape):
    return iota(shape, 1) < HD


def soften(scores):
    top = jnp.max(scores, axis=1, keepdims=True)
    return jnp.exp(scores - top).astype(BF), top


def ones_and_values(kv):
    return jnp.where(lanes_low(kv.shape), jnp.ones_like(kv), kv)


def merge(a, a_top, b, b_top):
    top = jnp.maximum(a_top, b_top)
    return a * jnp.exp(a_top - top) + b * jnp.exp(b_top - top), top


def spread(part, w):
    pieces = []
    for j in range(NX):
        pieces += [part[j * w : (j + 1) * w]] * 4
    return jnp.concatenate(pieces, axis=0)


def quotient(num, low_side):
    turned = pltpu.roll(num, HD, 1)
    return turned / num if low_side else num / turned


def order_of(y, z):
    return (8 * z + 7 * jnp.minimum(y, 2) + y // 3) * 4 + y


def kernel(
    qkv, offs, out,
    xin, perm, qs, kvs, kvrel, qr, qz, kv, k1s, q2s, k2, k3own, k3, osm, sm, n0, t0, n1, t1, outp,
    in_sem, own_sem, o_send, o_recv, q_send, q_recv, s_send, s_recv, u_send, u_recv, r_send, r_recv,
    c_send, c_recv, l2_send, l2_recv, l3_send, l3_recv, f_send, f_recv, ready,
):
    s = lax.axis_index("seq")
    x = lax.axis_index("head")
    core, z, y = s % 2, s // 2 % NZ, s // (2 * NZ)

    def along_x(k):
        return (s, (x + k) % NX)

    def along_seq(step):
        return ((y + step[0]) % NY * (2 * NZ) + (z + step[1]) % NZ * 2 + core, x)

    mine = order_of(y, z)

    def later(step):
        return order_of((y + step[0]) % NY, (z + step[1]) % NZ) > mine

    sibling = (s + 1 - 2 * core, x)
    barrier = pltpu.get_barrier_semaphore()
    near = [along_x(k) for k in (1, 2, 3)] + [sibling]
    for peer in near:
        pl.semaphore_signal(barrier, inc=1, device_id=peer, device_id_type=MESH)

    for step in L2_STEPS + L3_STEPS:

        @pl.when(later(step))
        def _():
            pl.semaphore_signal(barrier, inc=1, device_id=along_seq(step), device_id_type=MESH)

    own_offs = pltpu.make_async_copy(offs, osm, own_sem.at[2])
    own_offs.start()
    loads = [pltpu.make_async_copy(qkv.at[i], xin.at[i], in_sem.at[i]) for i in range(3)]
    for load in loads:
        load.start()

    n_later = jnp.int32(0)
    for step in L2_STEPS + L3_STEPS:
        n_later = n_later + jnp.where(later(step), 1, 0)
    n_earlier = len(L2_STEPS + L3_STEPS) - n_later

    sends = []

    def send(src, dst, send_sem, recv_sem, peer):
        copy = pltpu.make_async_remote_copy(
            src_ref=src, dst_ref=dst, send_sem=send_sem, recv_sem=recv_sem, device_id=peer, device_id_type=MESH
        )
        copy.start()
        sends.append(copy)
        return copy

    a, b = iota((ROWS, ROWS), 0), iota((ROWS, ROWS), 1)
    forth = jnp.where(b == source_row(a), 1.0, 0.0).astype(BF)
    perm[...] = forth
    low = lanes_low((ROWS, 128))
    low_half = lanes_low((128, 128))

    loads[0].wait()
    forth_scaled = forth * jnp.asarray(HD**-0.5, BF)
    for t in range(3):
        wide = dot(forth_scaled, xin[0, :, t * 256 : (t + 1) * 256])
        for u in range(4):
            head = 4 * t + u
            tile = wide[:, u // 2 * 128 : (u // 2 + 1) * 128]
            first, second = tile[:128], tile[128:]
            if u % 2 == 0:
                packed = jnp.where(low_half, first, pltpu.roll(second, HD, 1))
            else:
                packed = jnp.where(low_half, pltpu.roll(first, HD, 1), second)
            qs[head // GH, head % GH] = packed.astype(BF)

    own_offs.wait()
    for i in range(GH):
        sm[x, i] = osm[i]

    pl.semaphore_wait(barrier, len(near) + n_earlier)

    o_copies = [send(sm.at[x], sm.at[x], o_send.at[k - 1], o_recv.at[k - 1], along_x(k)) for k in (1, 2, 3)]

    def send_q(hh):
        return [
            send(qs.at[(x + k) % NX, hh], qr.at[hh, x], q_send.at[hh, k - 1], q_recv.at[hh, k - 1], along_x(k))
            for k in (1, 3, 2)
        ]

    q_copies = [send_q(0), send_q(1)]
    for step in L2_STEPS + L3_STEPS:

        @pl.when(jnp.logical_not(later(step)))
        def _():
            pl.semaphore_signal(ready, inc=1, device_id=along_seq(step), device_id_type=MESH)

    own_q = pltpu.make_async_copy(qs.at[x], qr.at[:, x], own_sem.at[0])
    own_q.start()

    loads[1].wait()
    loads[2].wait()
    for t in range(6):
        both = jnp.concatenate(
            [xin[1, :, t * 128 : (t + 1) * 128], xin[2, :, t * 128 : (t + 1) * 128]], axis=1
        )
        wide = dot(forth, both)
        keys, values = wide[:, :128], wide[:, 128:]
        even = jnp.where(low, keys, pltpu.roll(values, HD, 1))
        odd = jnp.where(low, pltpu.roll(keys, HD, 1), values)
        for head, packed in ((2 * t, even), (2 * t + 1, odd)):
            kvs[head // GH, head % GH] = packed.astype(BF)

    for copy in o_copies:
        copy.wait_recv()

    def send_rows(first, count, send_sem, recv_sem):
        own = pltpu.make_async_copy(
            kvrel.at[x, :, pl.ds(first, count), :], kv.at[:, x, pl.ds(first, count), :], own_sem.at[3 + first // 16]
        )
        own.start()
        return own, [
            send(
                kvrel.at[(x + k) % NX, :, pl.ds(first, count), :], kv.at[:, x, pl.ds(first, count), :],
                send_sem.at[k - 1], recv_sem.at[k - 1], along_x(k),
            )
            for k in (1, 3, 2)
        ]

    for g in range(NX):
        for hh in range(GH):
            b0, b1, b2, b3 = bits(sm[g, hh], (16, 128))
            parts = [kvs[g, hh, i * 16 : (i + 1) * 16, :] for i in range(16)]
            kvrel[g, hh, 0:16, :] = pick([pick(parts[i::4], b0, b1) for i in range(4)], b2, b3)
    own_s, s_copies = send_rows(0, 16, s_send, s_recv)
    for g in range(NX):
        for hh in range(GH):
            b0, b1, b2, b3 = bits(sm[g, hh], (16, 128))
            parts = [kvs[g, hh, i * 16 : (i + 1) * 16, :] for i in range(16)]
            parts = turn(turn(parts, b0, 4), b1, 8)
            parts[:4] = turn(turn(parts[:4], b2, 1), b3, 2)
            for i in range(1, 16):
                kvrel[g, hh, i * 16 : (i + 1) * 16, :] = parts[i]
    own_u, u_copies = send_rows(16, 48, u_send, u_recv)
    q_copies.append(send_q(2))
    r_copies = [
        [
            send(
                kvrel.at[(x + k) % NX, hh, pl.ds(64, 192), :], kv.at[hh, x, pl.ds(64, 192), :],
                r_send.at[hh, k - 1], r_recv.at[hh, k - 1], along_x(k),
            )
            for k in (1, 3, 2)
        ]
        for hh in range(GH)
    ]
    own_r = pltpu.make_async_copy(kvrel.at[x, :, pl.ds(64, 192), :], kv.at[:, x, pl.ds(64, 192), :], own_sem.at[1])
    own_r.start()

    digits = []
    for hh in range(GH):
        o = sm[x, hh]
        digits.append((o & 3, (o >> 2) & 3, (o >> 4) & 3))

    own_s.wait()
    for copy in s_copies:
        copy.wait_recv()
    e_row, e_col = iota((16, 64), 0), iota((16, 64), 1)
    for hh in range(GH):
        chosen = jnp.where(e_col == e_row // 4 * 16 + digits[hh][2] * 4 + e_row % 4, 1.0, 0.0).astype(BF)
        k3own[hh] = dot(chosen, kv[hh, :, 0:16, :].reshape(64, 128)).astype(BF)

    @pl.when(n_later > 0)
    def _():
        pl.semaphore_wait(ready, n_later)

    l3_copies = [
        send(k3own, k3.at[i], l3_send.at[i], l3_recv.at[i], along_seq(step)) for i, step in enumerate(L3_STEPS)
    ]
    l2_copies = [
        send(kv.at[:, :, pl.ds(0, 16), :], k2.at[i], l2_send.at[i], l2_recv.at[i], along_seq(step))
        for i, step in enumerate(L2_STEPS)
    ]
    own_u.wait()
    for copy in u_copies:
        copy.wait_recv()
    c_copy = send(kv.at[:, :, pl.ds(0, 64), :], k1s, c_send, c_recv, sibling)

    own_q.wait()
    for hh in range(GH):
        for copy in q_copies[hh]:
            copy.wait_recv()
        for j in range(NX):
            tile = qr[hh, j].astype(F32)
            qz[hh, j, 0:128, :] = jnp.where(low_half, tile, 0.0).astype(BF)
            qz[hh, j, 128:256, :] = jnp.where(low_half, pltpu.roll(tile, HD, 1), 0.0).astype(BF)

    c_copy.wait_recv()
    for hh in range(GH):
        b0, b1, b2, b3 = bits(sm[x, hh], (16, 128))
        q1 = []
        for j in range(NX):
            parts = [qz[hh, j, i * 16 : (i + 1) * 16, :] for i in range(16)]
            chosen = [pick(parts[i::4], b0, b1) for i in range(4)]
            q1 += chosen
            q2s[hh, j] = pick(chosen, b2, b3)
        q1 = jnp.concatenate(q1, axis=0)
        keys = jnp.concatenate([kv[hh, :, 0:64, :].reshape(256, 128), k1s[hh].reshape(256, 128)], axis=0)
        weights, top = soften(dot_t(q1, keys))
        n1[hh] = dot(weights, ones_and_values(keys))
        t1[hh] = top

    own_r.wait()
    for hh in range(GH):
        for copy in r_copies[hh]:
            copy.wait_recv()
        for seg in range(2):
            keys = kv[hh, 2 * seg : 2 * seg + 2].reshape(512, 128)
            values = ones_and_values(keys)
            for j in (2 * seg, 2 * seg + 1):
                weights, top = soften(dot_t(qz[hh, j], keys))
                num = dot(weights, values)
                n0[hh, j] = num
                t0[hh, j] = top
                value = quotient(num, hh % 2 == 0).astype(BF)
                if hh % 2 == 1:
                    value = jnp.where(low, outp[j, :, 0:128], value)
                outp[j, :, hh // 2 * 128 : (hh // 2 + 1) * 128] = value
        if hh == 0:
            for copy in l2_copies:
                copy.wait_recv()
            f2_copy = send(k2.at[pl.ds(0, N2)], k2.at[pl.ds(N2, N2)], f_send.at[0], f_recv.at[0], sibling)
        if hh == 1:
            for copy in l3_copies:
                copy.wait_recv()
            f3_copy = send(k3.at[pl.ds(0, N3)], k3.at[pl.ds(N3, N3)], f_send.at[1], f_recv.at[1], sibling)

    f2_copy.wait_recv()
    f3_copy.wait_recv()
    col = iota((64, 512), 1)
    row64 = iota((64, 1), 0)
    row256 = iota((ROWS, 1), 0)
    low16 = lanes_low((16, 128))
    for hh in range(GH):
        c1, c2, c3 = digits[hh]
        q2 = q2s[hh].reshape(64, 128)
        keys2 = jnp.concatenate(
            [kv[hh, :, 0:16, :].reshape(64, 128), k1s[hh, :, 0:16, :].reshape(64, 128)]
            + [k2[i, hh].reshape(64, 128) for i in range(2 * N2)],
            axis=0,
        )
        keys3 = jnp.concatenate([k3[i, hh] for i in range(2 * N3)], axis=0)
        values2 = ones_and_values(keys2)
        scores2 = dot_t(q2, keys2)
        weights2, top2 = soften(scores2)
        weights3, top3 = soften(
            jnp.concatenate([jnp.where(col % 16 // 4 == c3, scores2, LOW), dot_t(q2, keys3)], axis=1)
        )
        num3 = dot(weights3[:, :512], values2) + dot(weights3[:, 512:], ones_and_values(keys3))
        num2, top2 = merge(
            dot(weights2, values2), top2, num3, jnp.where(row64 % 16 // 4 == c3, top3, LOW)
        )
        num1, top1 = merge(
            n1[hh], t1[hh], spread(num2, 16), jnp.where(row256 % 64 // 16 == c2, spread(top2, 16), LOW)
        )
        b0, b1, _, _ = bits(sm[x, hh], (64, 128))
        part = jnp.concatenate(
            [pick([n0[hh, j, i * 64 : (i + 1) * 64, :] for i in range(4)], b0, b1) for j in range(NX)], axis=0
        )
        b0, b1, _, _ = bits(sm[x, hh], (64, 1))
        part_top = jnp.concatenate(
            [pick([t0[hh, j, i * 64 : (i + 1) * 64, :] for i in range(4)], b0, b1) for j in range(NX)], axis=0
        )
        num, _ = merge(part, part_top, num1, top1)
        value = quotient(num, hh % 2 == 0).astype(BF)
        place = jnp.zeros((16, 128), jnp.int32) + c1
        side = [low16, jnp.logical_not(low16), low16][hh]
        masks = [(place == i) & side for i in range(4)]
        lanes = slice(hh // 2 * 128, (hh // 2 + 1) * 128)
        for j in range(NX):
            for i in range(16):
                new = value[j * 64 + i % 4 * 16 : j * 64 + i % 4 * 16 + 16]
                rows = slice(i * 16, (i + 1) * 16)
                outp[j, rows, lanes] = jnp.where(masks[i // 4], new, outp[j, rows, lanes])
    for j in range(NX):
        final = lax.dot_general(
            outp[j], perm[...], (((0,), (0,)), ((), ())), preferred_element_type=F32
        )
        out[:, j * ROWS : (j + 1) * ROWS] = final[: GH * HD].astype(BF)

    for copy in sends:
        copy.wait_send()


def per_device(qkv, offsets):
    dma = pltpu.SemaphoreType.DMA
    turned = pl.pallas_call(
        kernel,
        out_shape=jax.ShapeDtypeStruct((GH * HD, NX * ROWS), BF),
        in_specs=[pl.BlockSpec(memory_space=pltpu.HBM), pl.BlockSpec(memory_space=pltpu.HBM)],
        out_specs=pl.BlockSpec(memory_space=pltpu.VMEM),
        scratch_shapes=[
            pltpu.VMEM((3, ROWS, 768), BF),
            pltpu.VMEM((ROWS, ROWS), BF),
            pltpu.VMEM((NX, GH, 128, 128), BF),
            pltpu.VMEM((NX, GH, ROWS, 128), BF),
            pltpu.VMEM((NX, GH, ROWS, 128), BF),
            pltpu.VMEM((GH, NX, 128, 128), BF),
            pltpu.VMEM((GH, NX, ROWS, 128), BF),
            pltpu.VMEM((GH, NX, ROWS, 128), BF),
            pltpu.VMEM((GH, NX, 64, 128), BF),
            pltpu.VMEM((GH, NX, 16, 128), BF),
            pltpu.VMEM((2 * N2, GH, NX, 16, 128), BF),
            pltpu.VMEM((GH, 16, 128), BF),
            pltpu.VMEM((2 * N3, GH, 16, 128), BF),
            pltpu.SMEM((GH,), jnp.int32),
            pltpu.SMEM((NX, 128), jnp.int32),
            pltpu.VMEM((GH, NX, ROWS, 128), F32),
            pltpu.VMEM((GH, NX, ROWS, 1), F32),
            pltpu.VMEM((GH, ROWS, 128), F32),
            pltpu.VMEM((GH, ROWS, 1), F32),
            pltpu.VMEM((NX, ROWS, 256), BF),
            dma((3,)), dma((5,)), dma((3,)), dma((3,)), dma((GH, 3)), dma((GH, 3)), dma((3,)), dma((3,)),
            dma((3,)), dma((3,)), dma((GH, 3)), dma((GH, 3)), dma, dma, dma((N2,)), dma((N2,)), dma((N3,)), dma((N3,)),
            dma((2,)), dma((2,)),
            pltpu.SemaphoreType.REGULAR,
        ],
        compiler_params=pltpu.CompilerParams(
            collective_id=0, has_side_effects=True, vmem_limit_bytes=40 * 2**20
        ),
        cost_estimate=pl.CostEstimate(flops=10**9, bytes_accessed=2 * 10**6, transcendentals=2 * 10**6),
    )(qkv, offsets)
    return turned.T


def solution(mesh):
    return jax.shard_map(
        per_device,
        mesh=mesh,
        in_specs=(P(None, ("seq", "head"), None), P("head")),
        out_specs=P("seq", "head"),
        check_vma=False,
    )
```

time: 34 us -> 27.4 us (0.81)
  Pallas kernels: 31 us -> 24.5 us
    pallas_call x1, Pallas kernels: 31 us -> 24.5 us  [per_device(): pl.pallas_call(kernel, out_shape=jax.ShapeDtypeStruct((GH * HD, NX * ROWS...]
    pallas_call x1 -> x0, local copies, waits for them, and re-layouts: 0.94 us -> none  [per_device(): pl.pallas_call(kernel, out_shape=jax.ShapeDtypeStruct((NX * ROWS, GH * HD...]
    unnamed x4 -> x5, local copies, waits for them, and re-layouts: 1.92 us -> 2.67 us
where the time goes in v2:
time: 27.4 us; the launch traced here: 27.2 us
  Pallas kernels  24.5 us (89%)
  local copies, waits for them, and re-layouts  2.67 us (10%)
    pallas_call x1, Pallas kernels, per_device(): pl.pallas_call(kernel, out_shape=jax.ShapeDtypeStruct((GH * HD, NX * ROWS...  24.5 us
    unnamed x5, local copies, waits for them, and re-layouts  2.67 us

profile of v2, /device:TPU:1, one launch (start us, length us, event | category | flops | bytes accessed | tf_op | source)
XLA Modules:
  0.0 27.2 jit_solution(12830249875880430135)
XLA Ops:
  0.0 0.0 copy-start
  0.0 1.3 %copy-done = bf16[3,256,768]{2,1,0:T(8,128)(2,1)S(1)} copy-done((bf16[3,256,768]{2,1,0:T(8,128)(2,1)S(1)}, bf16[3,256,768]{2,1,0:T(8,128)(2,1)}, u32[]{:S(2)}) %copy-start) | copy-done | bytes 1179672
  1.3 0.0 copy-start.1
  1.3 0.7 %copy-done.1 = s32[3]{0:T(128)S(1)} copy-done((s32[3]{0:T(128)S(1)}, s32[3]{0:T(128)}, u32[]{:S(2)}) %copy-start.1) | copy-done | bytes 36
  1.9 24.5 %shard_map.28 = bf16[192,1024]{1,0:T(8,128)(2,1)S(1)} custom-call(bf16[3,256,768]{2,1,0:T(8,128)(2,1)S(1)} %copy-done, s32[3]{0:T(128)S(1)} %copy-done.1), custom_call_target="tpu_custom_call" | custom-call | flops 1000000000 | bytes 2000000 | tf_op jit(solution)/shard_map/pallas_call | solution.py:380
  26.5 0.7 %copy.4 = bf16[1024,192]{0,1:T(8,128)(2,1)} copy(bf16[1024,192]{0,1:T(8,128)(2,1)S(1)} %bitcast.1) | data formatting | bytes 786432
Async XLA Ops:
  0.0 1.3 %copy-start = (bf16[3,256,768]{2,1,0:T(8,128)(2,1)S(1)}, bf16[3,256,768]{2,1,0:T(8,128)(2,1)}, u32[]{:S(2)}) copy-start(bf16[3,256,768]{2,1,0:T(8,128)(2,1)} %qkv.1) | copy-start | bytes 3538948
  1.3 0.7 %copy-start.1 = (s32[3]{0:T(128)S(1)}, s32[3]{0:T(128)}, u32[]{:S(2)}) copy-start(s32[3]{0:T(128)} %offs.1) | copy-start | bytes 40

commit v3 on v2

--- a/solution.py
+++ b/solution.py
@@ -34,7 +34,7 @@
 
 
 def source_row(i):
-    return (i % 4) * 64 + (i // 4 % 4) * 16 + (i // 16 % 4) * 4 + i // 64
+    return ((i & 3) << 6) | ((i & 12) << 2) | ((i & 48) >> 2) | (i >> 6)
 
 
 def bits(o, shape):
@@ -81,33 +81,34 @@
 
 
 def order_of(y, z):
-    return (8 * z + 7 * jnp.minimum(y, 2) + y // 3) * 4 + y
+    return (8 * z + 7 * jnp.minimum(y, 2) + jnp.where(y == 3, 1, 0)) * 4 + y
 
 
 def kernel(
     qkv, offs, out,
-    xin, perm, qs, kvs, kvrel, qr, qz, kv, k1s, q2s, k2, k3own, k3, osm, sm, n0, t0, n1, t1, outp,
+    xin, perm, qs, kvs, kvrel, qr, qz, kv, k1s, q2s, k2, k3own, k3, osm, sm, n0, t0, n1, t1, s2, v2, n2, t2, outp,
     in_sem, own_sem, o_send, o_recv, q_send, q_recv, s_send, s_recv, u_send, u_recv, r_send, r_recv,
     c_send, c_recv, l2_send, l2_recv, l3_send, l3_recv, f_send, f_recv, ready,
 ):
     s = lax.axis_index("seq")
     x = lax.axis_index("head")
-    core, z, y = s % 2, s // 2 % NZ, s // (2 * NZ)
+    core, z, y = lax.rem(s, 2), lax.rem(lax.div(s, 2), NZ), lax.div(s, 2 * NZ)
 
     def along_x(k):
-        return (s, (x + k) % NX)
+        return (s, lax.rem(x + k, NX))
 
     def along_seq(step):
-        return ((y + step[0]) % NY * (2 * NZ) + (z + step[1]) % NZ * 2 + core, x)
+        return (lax.rem(y + step[0], NY) * (2 * NZ) + lax.rem(z + step[1], NZ) * 2 + core, x)
 
     mine = order_of(y, z)
 
     def later(step):
-        return order_of((y + step[0]) % NY, (z + step[1]) % NZ) > mine
+        return order_of(lax.rem(y + step[0], NY), lax.rem(z + step[1], NZ)) > mine
 
     sibling = (s + 1 - 2 * core, x)
     barrier = pltpu.get_barrier_semaphore()
-    near = [along_x(k) for k in (1, 2, 3)] + [sibling]
+    other = [(s + 1 - 2 * core, lax.rem(x + k, NX)) for k in (1, 2, 3)]
+    near = [along_x(k) for k in (1, 2, 3)] + [sibling] + other
     for peer in near:
         pl.semaphore_signal(barrier, inc=1, device_id=peer, device_id_type=MESH)
 
@@ -143,6 +144,28 @@
     perm[...] = forth
     low = lanes_low((ROWS, 128))
     low_half = lanes_low((128, 128))
+
+    own_offs.wait()
+    for i in range(GH):
+        sm[x, i] = osm[i]
+    pl.semaphore_wait(barrier, len(near) + n_earlier)
+    o_copies = [
+        [
+            pltpu.make_async_remote_copy(
+                src_ref=sm.at[x], dst_ref=sm.at[x], send_sem=o_send.at[c, k - 1], recv_sem=o_recv.at[k - 1],
+                device_id=(s - core + c, lax.rem(x + k, NX)), device_id_type=MESH,
+            )
+            for k in (1, 2, 3)
+        ]
+        for c in (0, 1)
+    ]
+
+    @pl.when(core == 1)
+    def _():
+        for k in (3, 1, 2):
+            for c in (0, 1):
+                o_copies[c][k - 1].start()
+
 
     loads[0].wait()
     forth_scaled = forth * jnp.asarray(HD**-0.5, BF)
@@ -158,21 +181,13 @@
                 packed = jnp.where(low_half, pltpu.roll(first, HD, 1), second)
             qs[head // GH, head % GH] = packed.astype(BF)
 
-    own_offs.wait()
-    for i in range(GH):
-        sm[x, i] = osm[i]
-
-    pl.semaphore_wait(barrier, len(near) + n_earlier)
-
-    o_copies = [send(sm.at[x], sm.at[x], o_send.at[k - 1], o_recv.at[k - 1], along_x(k)) for k in (1, 2, 3)]
-
     def send_q(hh):
         return [
-            send(qs.at[(x + k) % NX, hh], qr.at[hh, x], q_send.at[hh, k - 1], q_recv.at[hh, k - 1], along_x(k))
+            send(qs.at[lax.rem(x + k, NX), hh], qr.at[hh, x], q_send.at[hh, k - 1], q_recv.at[hh, k - 1], along_x(k))
             for k in (1, 3, 2)
         ]
 
-    q_copies = [send_q(0), send_q(1)]
+    q_copies = [send_q(0)]
     for step in L2_STEPS + L3_STEPS:
 
         @pl.when(jnp.logical_not(later(step)))
@@ -195,28 +210,32 @@
         for head, packed in ((2 * t, even), (2 * t + 1, odd)):
             kvs[head // GH, head % GH] = packed.astype(BF)
 
-    for copy in o_copies:
-        copy.wait_recv()
-
-    def send_rows(first, count, send_sem, recv_sem):
-        own = pltpu.make_async_copy(
-            kvrel.at[x, :, pl.ds(first, count), :], kv.at[:, x, pl.ds(first, count), :], own_sem.at[3 + first // 16]
-        )
-        own.start()
-        return own, [
-            send(
-                kvrel.at[(x + k) % NX, :, pl.ds(first, count), :], kv.at[:, x, pl.ds(first, count), :],
-                send_sem.at[k - 1], recv_sem.at[k - 1], along_x(k),
-            )
-            for k in (1, 3, 2)
-        ]
-
-    for g in range(NX):
+    def pick_first(g):
         for hh in range(GH):
             b0, b1, b2, b3 = bits(sm[g, hh], (16, 128))
             parts = [kvs[g, hh, i * 16 : (i + 1) * 16, :] for i in range(16)]
             kvrel[g, hh, 0:16, :] = pick([pick(parts[i::4], b0, b1) for i in range(4)], b2, b3)
-    own_s, s_copies = send_rows(0, 16, s_send, s_recv)
+
+    def send_rows_to(k, first, count, send_sem, recv_sem):
+        return send(
+            kvrel.at[lax.rem(x + k, NX), :, pl.ds(first, count), :], kv.at[:, x, pl.ds(first, count), :],
+            send_sem.at[k - 1], recv_sem.at[k - 1], along_x(k),
+        )
+
+    def keep_rows(first, count, sem):
+        own = pltpu.make_async_copy(
+            kvrel.at[x, :, pl.ds(first, count), :], kv.at[:, x, pl.ds(first, count), :], sem
+        )
+        own.start()
+        return own
+
+    pick_first(x)
+    own_s = keep_rows(0, 16, own_sem.at[3])
+    s_copies = []
+    for k in (1, 3, 2):
+        o_copies[0][3 - k].wait_recv()
+        pick_first(lax.rem(x + k, NX))
+        s_copies.append(send_rows_to(k, 0, 16, s_send, s_recv))
     for g in range(NX):
         for hh in range(GH):
             b0, b1, b2, b3 = bits(sm[g, hh], (16, 128))
@@ -225,20 +244,20 @@
             parts[:4] = turn(turn(parts[:4], b2, 1), b3, 2)
             for i in range(1, 16):
                 kvrel[g, hh, i * 16 : (i + 1) * 16, :] = parts[i]
-    own_u, u_copies = send_rows(16, 48, u_send, u_recv)
-    q_copies.append(send_q(2))
+    u_copies = [send_rows_to(k, 16, 48, u_send, u_recv) for k in (1, 3, 2)]
+    own_u = keep_rows(16, 48, own_sem.at[4])
+    q_copies += [send_q(1), send_q(2)]
     r_copies = [
         [
             send(
-                kvrel.at[(x + k) % NX, hh, pl.ds(64, 192), :], kv.at[hh, x, pl.ds(64, 192), :],
+                kvrel.at[lax.rem(x + k, NX), hh, pl.ds(64, 192), :], kv.at[hh, x, pl.ds(64, 192), :],
                 r_send.at[hh, k - 1], r_recv.at[hh, k - 1], along_x(k),
             )
             for k in (1, 3, 2)
         ]
         for hh in range(GH)
     ]
-    own_r = pltpu.make_async_copy(kvrel.at[x, :, pl.ds(64, 192), :], kv.at[:, x, pl.ds(64, 192), :], own_sem.at[1])
-    own_r.start()
+    own_r = keep_rows(64, 192, own_sem.at[1])
 
     digits = []
     for hh in range(GH):
@@ -250,7 +269,7 @@
         copy.wait_recv()
     e_row, e_col = iota((16, 64), 0), iota((16, 64), 1)
     for hh in range(GH):
-        chosen = jnp.where(e_col == e_row // 4 * 16 + digits[hh][2] * 4 + e_row % 4, 1.0, 0.0).astype(BF)
+        chosen = jnp.where(e_col == ((e_row & 12) << 2) + digits[hh][2] * 4 + (e_row & 3), 1.0, 0.0).astype(BF)
         k3own[hh] = dot(chosen, kv[hh, :, 0:16, :].reshape(64, 128)).astype(BF)
 
     @pl.when(n_later > 0)
@@ -279,6 +298,7 @@
             qz[hh, j, 128:256, :] = jnp.where(low_half, pltpu.roll(tile, HD, 1), 0.0).astype(BF)
 
     c_copy.wait_recv()
+    keys, values, scores = [], [], []
     for hh in range(GH):
         b0, b1, b2, b3 = bits(sm[x, hh], (16, 128))
         q1 = []
@@ -288,24 +308,27 @@
             q1 += chosen
             q2s[hh, j] = pick(chosen, b2, b3)
         q1 = jnp.concatenate(q1, axis=0)
-        keys = jnp.concatenate([kv[hh, :, 0:64, :].reshape(256, 128), k1s[hh].reshape(256, 128)], axis=0)
-        weights, top = soften(dot_t(q1, keys))
-        n1[hh] = dot(weights, ones_and_values(keys))
-        t1[hh] = top
+        keys.append(jnp.concatenate([kv[hh, :, 0:64, :].reshape(256, 128), k1s[hh].reshape(256, 128)], axis=0))
+        scores.append(dot_t(q1, keys[hh]))
+    soft = [soften(scores[hh]) for hh in range(GH)]
+    for hh in range(GH):
+        n1[hh] = dot(soft[hh][0], ones_and_values(keys[hh]))
+        t1[hh] = soft[hh][1]
 
     own_r.wait()
     for hh in range(GH):
         for copy in r_copies[hh]:
             copy.wait_recv()
-        for seg in range(2):
-            keys = kv[hh, 2 * seg : 2 * seg + 2].reshape(512, 128)
-            values = ones_and_values(keys)
-            for j in (2 * seg, 2 * seg + 1):
-                weights, top = soften(dot_t(qz[hh, j], keys))
-                num = dot(weights, values)
-                n0[hh, j] = num
-                t0[hh, j] = top
-                value = quotient(num, hh % 2 == 0).astype(BF)
+        keys = [kv[hh, 2 * seg : 2 * seg + 2].reshape(512, 128) for seg in range(2)]
+        values = [ones_and_values(keys[seg]) for seg in range(2)]
+        for pair in ((0, 2), (1, 3)):
+            scores = [dot_t(qz[hh, j], keys[j // 2]) for j in pair]
+            soft = [soften(scores[i]) for i in range(2)]
+            nums = [dot(soft[i][0], values[pair[i] // 2]) for i in range(2)]
+            for i, j in enumerate(pair):
+                n0[hh, j] = nums[i]
+                t0[hh, j] = soft[i][1]
+                value = quotient(nums[i], hh % 2 == 0).astype(BF)
                 if hh % 2 == 1:
                     value = jnp.where(low, outp[j, :, 0:128], value)
                 outp[j, :, hh // 2 * 128 : (hh // 2 + 1) * 128] = value
@@ -319,33 +342,50 @@
             f3_copy = send(k3.at[pl.ds(0, N3)], k3.at[pl.ds(N3, N3)], f_send.at[1], f_recv.at[1], sibling)
 
     f2_copy.wait_recv()
+    scores = []
+    for hh in range(GH):
+        keys2 = jnp.concatenate(
+            [kv[hh, :, 0:16, :].reshape(64, 128), k1s[hh, :, 0:16, :].reshape(64, 128)]
+            + [k2[i, hh].reshape(64, 128) for i in range(2 * N2)],
+            axis=0,
+        )
+        scores.append(dot_t(q2s[hh].reshape(64, 128), keys2))
+        s2[hh] = scores[hh]
+        v2[hh] = ones_and_values(keys2)
+    soft = [soften(scores[hh]) for hh in range(GH)]
+    for hh in range(GH):
+        n2[hh] = dot(soft[hh][0], v2[hh])
+        t2[hh] = soft[hh][1]
+
     f3_copy.wait_recv()
     col = iota((64, 512), 1)
     row64 = iota((64, 1), 0)
     row256 = iota((ROWS, 1), 0)
     low16 = lanes_low((16, 128))
-    for hh in range(GH):
-        c1, c2, c3 = digits[hh]
-        q2 = q2s[hh].reshape(64, 128)
-        keys2 = jnp.concatenate(
-            [kv[hh, :, 0:16, :].reshape(64, 128), k1s[hh, :, 0:16, :].reshape(64, 128)]
-            + [k2[i, hh].reshape(64, 128) for i in range(2 * N2)],
-            axis=0,
-        )
-        keys3 = jnp.concatenate([k3[i, hh] for i in range(2 * N3)], axis=0)
-        values2 = ones_and_values(keys2)
-        scores2 = dot_t(q2, keys2)
-        weights2, top2 = soften(scores2)
-        weights3, top3 = soften(
-            jnp.concatenate([jnp.where(col % 16 // 4 == c3, scores2, LOW), dot_t(q2, keys3)], axis=1)
-        )
-        num3 = dot(weights3[:, :512], values2) + dot(weights3[:, 512:], ones_and_values(keys3))
-        num2, top2 = merge(
-            dot(weights2, values2), top2, num3, jnp.where(row64 % 16 // 4 == c3, top3, LOW)
-        )
-        num1, top1 = merge(
-            n1[hh], t1[hh], spread(num2, 16), jnp.where(row256 % 64 // 16 == c2, spread(top2, 16), LOW)
-        )
+    keys = [jnp.concatenate([k3[i, hh] for i in range(2 * N3)], axis=0) for hh in range(GH)]
+    scores = [dot_t(q2s[hh].reshape(64, 128), keys[hh]) for hh in range(GH)]
+    soft = [
+        soften(jnp.concatenate([jnp.where(((col >> 2) & 3) == digits[hh][2], s2[hh], LOW), scores[hh]], axis=1))
+        for hh in range(GH)
+    ]
+    num3 = [
+        dot(soft[hh][0][:, :512], v2[hh]) + dot(soft[hh][0][:, 512:], ones_and_values(keys[hh]))
+        for hh in range(GH)
+    ]
+    both = [
+        merge(n2[hh], t2[hh], num3[hh], jnp.where(((row64 >> 2) & 3) == digits[hh][2], soft[hh][1], LOW))
+        for hh in range(GH)
+    ]
+    both = [
+        merge(
+            n1[hh], t1[hh], spread(both[hh][0], 16),
+            jnp.where(((row256 >> 4) & 3) == digits[hh][1], spread(both[hh][1], 16), LOW),
+        )
+        for hh in range(GH)
+    ]
+    for hh in range(GH):
+        c1 = digits[hh][0]
+        num1, top1 = both[hh]
         b0, b1, _, _ = bits(sm[x, hh], (64, 128))
         part = jnp.concatenate(
             [pick([n0[hh, j, i * 64 : (i + 1) * 64, :] for i in range(4)], b0, b1) for j in range(NX)], axis=0
@@ -373,6 +413,11 @@
 
     for copy in sends:
         copy.wait_send()
+
+    @pl.when(core == 1)
+    def _():
+        for copy in o_copies[0] + o_copies[1]:
+            copy.wait_send()
 
 
 def per_device(qkv, offsets):
@@ -402,8 +447,12 @@
             pltpu.VMEM((GH, NX, ROWS, 1), F32),
             pltpu.VMEM((GH, ROWS, 128), F32),
             pltpu.VMEM((GH, ROWS, 1), F32),
+            pltpu.VMEM((GH, 64, 512), F32),
+            pltpu.VMEM((GH, 512, 128), BF),
+            pltpu.VMEM((GH, 64, 128), F32),
+            pltpu.VMEM((GH, 64, 1), F32),
             pltpu.VMEM((NX, ROWS, 256), BF),
-            dma((3,)), dma((5,)), dma((3,)), dma((3,)), dma((GH, 3)), dma((GH, 3)), dma((3,)), dma((3,)),
+            dma((3,)), dma((8,)), dma((2, 3)), dma((3,)), dma((GH, 3)), dma((GH, 3)), dma((3,)), dma((3,)),
             dma((3,)), dma((3,)), dma((GH, 3)), dma((GH, 3)), dma, dma, dma((N2,)), dma((N2,)), dma((N3,)), dma((N3,)),
             dma((2,)), dma((2,)),
             pltpu.SemaphoreType.REGULAR,
@@ -412,7 +461,7 @@
             collective_id=0, has_side_effects=True, vmem_limit_bytes=40 * 2**20
         ),
         cost_estimate=pl.CostEstimate(flops=10**9, bytes_accessed=2 * 10**6, transcendentals=2 * 10**6),
-    )(qkv, offsets)
+    )(pltpu.with_memory_space_constraint(qkv, pltpu.HBM), pltpu.with_memory_space_constraint(offsets, pltpu.HBM))
     return turned.T
 
 

time: 27.4 us -> 24.9 us (0.909)
  local copies, waits for them, and re-layouts: 2.67 us -> 0.75 us
  Pallas kernels: 24.5 us -> 24 us
    unnamed x5 -> x1, local copies, waits for them, and re-layouts: 2.67 us -> 0.75 us
    pallas_call x1, Pallas kernels: 24.5 us -> 24 us  [per_device(): pl.pallas_call(kernel, out_shape=jax.ShapeDtypeStruct((GH * HD, NX * ROWS...]
where the time goes in v3:
time: 24.9 us; the launch traced here: 24.7 us
  Pallas kernels  24 us (96%)
  local copies, waits for them, and re-layouts  0.75 us (3%)
    pallas_call x1, Pallas kernels, per_device(): pl.pallas_call(kernel, out_shape=jax.ShapeDtypeStruct((GH * HD, NX * ROWS...  24 us
    unnamed x1, local copies, waits for them, and re-layouts  0.75 us

profile of v3, /device:TPU:1, one launch (start us, length us, event | category | flops | bytes accessed | tf_op | source)
XLA Modules:
  0.0 24.7 jit_solution(2477573909349295037)
XLA Ops:
  0.0 24.0 %shard_map.28 = bf16[192,1024]{1,0:T(8,128)(2,1)S(1)} custom-call(bf16[3,256,768]{2,1,0:T(8,128)(2,1)} %qkv.1, s32[3]{0:T(128)} %offs.1), custom_call_target="tpu_custom_call" | custom-call | flops 1000000000 | bytes 2000000 | tf_op jit(solution)/shard_map/pallas_call | solution.py:425
  24.0 0.7 %copy.4 = bf16[1024,192]{0,1:T(8,128)(2,1)} copy(bf16[1024,192]{0,1:T(8,128)(2,1)S(1)} %bitcast.1) | data formatting | bytes 786432

commit v4 on v3

--- a/solution.py
+++ b/solution.py
@@ -68,25 +68,19 @@
     return a * jnp.exp(a_top - top) + b * jnp.exp(b_top - top), top
 
 
-def spread(part, w):
-    pieces = []
-    for j in range(NX):
-        pieces += [part[j * w : (j + 1) * w]] * 4
-    return jnp.concatenate(pieces, axis=0)
-
-
 def quotient(num, low_side):
     turned = pltpu.roll(num, HD, 1)
     return turned / num if low_side else num / turned
 
 
 def order_of(y, z):
-    return (8 * z + 7 * jnp.minimum(y, 2) + jnp.where(y == 3, 1, 0)) * 4 + y
+    corner = jnp.where((z == 3) & (y == 0), 4, 0) + jnp.where((z == 0) & (y == 3), 6, 0)
+    return (8 * z + 7 * jnp.minimum(y, 2) + jnp.where(y == 3, 1, 0) - corner) * 4 + y
 
 
 def kernel(
     qkv, offs, out,
-    xin, perm, qs, kvs, kvrel, qr, qz, kv, k1s, q2s, k2, k3own, k3, osm, sm, n0, t0, n1, t1, s2, v2, n2, t2, outp,
+    xin, perm, qs, kvs, kvrel, qr, qz, kv, k1s, q2s, k2, k3own, k3, osm, sm, n0, t0, n1, t1, nm, tm, s2, v2, n2, t2, outp,
     in_sem, own_sem, o_send, o_recv, q_send, q_recv, s_send, s_recv, u_send, u_recv, r_send, r_recv,
     c_send, c_recv, l2_send, l2_recv, l3_send, l3_recv, f_send, f_recv, ready,
 ):
@@ -144,6 +138,20 @@
     perm[...] = forth
     low = lanes_low((ROWS, 128))
     low_half = lanes_low((128, 128))
+
+    loads[0].wait()
+    forth_scaled = forth * jnp.asarray(HD**-0.5, BF)
+    for t in range(3):
+        wide = dot(forth_scaled, xin[0, :, t * 256 : (t + 1) * 256])
+        for u in range(4):
+            head = 4 * t + u
+            tile = wide[:, u // 2 * 128 : (u // 2 + 1) * 128]
+            first, second = tile[:128], tile[128:]
+            if u % 2 == 0:
+                packed = jnp.where(low_half, first, pltpu.roll(second, HD, 1))
+            else:
+                packed = jnp.where(low_half, pltpu.roll(first, HD, 1), second)
+            qs[head // GH, head % GH] = packed.astype(BF)
 
     own_offs.wait()
     for i in range(GH):
@@ -167,27 +175,13 @@
                 o_copies[c][k - 1].start()
 
 
-    loads[0].wait()
-    forth_scaled = forth * jnp.asarray(HD**-0.5, BF)
-    for t in range(3):
-        wide = dot(forth_scaled, xin[0, :, t * 256 : (t + 1) * 256])
-        for u in range(4):
-            head = 4 * t + u
-            tile = wide[:, u // 2 * 128 : (u // 2 + 1) * 128]
-            first, second = tile[:128], tile[128:]
-            if u % 2 == 0:
-                packed = jnp.where(low_half, first, pltpu.roll(second, HD, 1))
-            else:
-                packed = jnp.where(low_half, pltpu.roll(first, HD, 1), second)
-            qs[head // GH, head % GH] = packed.astype(BF)
-
     def send_q(hh):
         return [
             send(qs.at[lax.rem(x + k, NX), hh], qr.at[hh, x], q_send.at[hh, k - 1], q_recv.at[hh, k - 1], along_x(k))
             for k in (1, 3, 2)
         ]
 
-    q_copies = [send_q(0)]
+    q_copies = [send_q(0), send_q(1)]
     for step in L2_STEPS + L3_STEPS:
 
         @pl.when(jnp.logical_not(later(step)))
@@ -246,7 +240,7 @@
                 kvrel[g, hh, i * 16 : (i + 1) * 16, :] = parts[i]
     u_copies = [send_rows_to(k, 16, 48, u_send, u_recv) for k in (1, 3, 2)]
     own_u = keep_rows(16, 48, own_sem.at[4])
-    q_copies += [send_q(1), send_q(2)]
+    q_copies += [send_q(2)]
     r_copies = [
         [
             send(
@@ -276,12 +270,12 @@
     def _():
         pl.semaphore_wait(ready, n_later)
 
-    l3_copies = [
-        send(k3own, k3.at[i], l3_send.at[i], l3_recv.at[i], along_seq(step)) for i, step in enumerate(L3_STEPS)
-    ]
     l2_copies = [
         send(kv.at[:, :, pl.ds(0, 16), :], k2.at[i], l2_send.at[i], l2_recv.at[i], along_seq(step))
         for i, step in enumerate(L2_STEPS)
+    ]
+    l3_copies = [
+        send(k3own, k3.at[i], l3_send.at[i], l3_recv.at[i], along_seq(step)) for i, step in enumerate(L3_STEPS)
     ]
     own_u.wait()
     for copy in u_copies:
@@ -316,6 +310,7 @@
         t1[hh] = soft[hh][1]
 
     own_r.wait()
+    low16 = lanes_low((16, 128))
     for hh in range(GH):
         for copy in r_copies[hh]:
             copy.wait_recv()
@@ -332,6 +327,27 @@
                 if hh % 2 == 1:
                     value = jnp.where(low, outp[j, :, 0:128], value)
                 outp[j, :, hh // 2 * 128 : (hh // 2 + 1) * 128] = value
+        b0, b1, _, _ = bits(sm[x, hh], (64, 128))
+        part = jnp.concatenate(
+            [pick([n0[hh, j, i * 64 : (i + 1) * 64, :] for i in range(4)], b0, b1) for j in range(NX)], axis=0
+        )
+        b0, b1, _, _ = bits(sm[x, hh], (64, 1))
+        part_top = jnp.concatenate(
+            [pick([t0[hh, j, i * 64 : (i + 1) * 64, :] for i in range(4)], b0, b1) for j in range(NX)], axis=0
+        )
+        num, top = merge(part, part_top, n1[hh], t1[hh])
+        nm[hh] = num
+        tm[hh] = top
+        value = quotient(num, hh % 2 == 0).astype(BF)
+        place = jnp.zeros((16, 128), jnp.int32) + digits[hh][0]
+        side = [low16, jnp.logical_not(low16), low16][hh]
+        masks = [(place == i) & side for i in range(4)]
+        lanes = slice(hh // 2 * 128, (hh // 2 + 1) * 128)
+        for j in range(NX):
+            for i in range(16):
+                new = value[j * 64 + i % 4 * 16 : j * 64 + i % 4 * 16 + 16]
+                rows = slice(i * 16, (i + 1) * 16)
+                outp[j, rows, lanes] = jnp.where(masks[i // 4], new, outp[j, rows, lanes])
         if hh == 0:
             for copy in l2_copies:
                 copy.wait_recv()
@@ -340,28 +356,25 @@
             for copy in l3_copies:
                 copy.wait_recv()
             f3_copy = send(k3.at[pl.ds(0, N3)], k3.at[pl.ds(N3, N3)], f_send.at[1], f_recv.at[1], sibling)
-
-    f2_copy.wait_recv()
-    scores = []
-    for hh in range(GH):
-        keys2 = jnp.concatenate(
-            [kv[hh, :, 0:16, :].reshape(64, 128), k1s[hh, :, 0:16, :].reshape(64, 128)]
-            + [k2[i, hh].reshape(64, 128) for i in range(2 * N2)],
-            axis=0,
-        )
-        scores.append(dot_t(q2s[hh].reshape(64, 128), keys2))
-        s2[hh] = scores[hh]
-        v2[hh] = ones_and_values(keys2)
-    soft = [soften(scores[hh]) for hh in range(GH)]
-    for hh in range(GH):
-        n2[hh] = dot(soft[hh][0], v2[hh])
-        t2[hh] = soft[hh][1]
+            f2_copy.wait_recv()
+            scores = []
+            for hb in range(GH):
+                keys2 = jnp.concatenate(
+                    [kv[hb, :, 0:16, :].reshape(64, 128), k1s[hb, :, 0:16, :].reshape(64, 128)]
+                    + [k2[i, hb].reshape(64, 128) for i in range(2 * N2)],
+                    axis=0,
+                )
+                scores.append(dot_t(q2s[hb].reshape(64, 128), keys2))
+                s2[hb] = scores[hb]
+                v2[hb] = ones_and_values(keys2)
+            soft = [soften(scores[hb]) for hb in range(GH)]
+            for hb in range(GH):
+                n2[hb] = dot(soft[hb][0], v2[hb])
+                t2[hb] = soft[hb][1]
 
     f3_copy.wait_recv()
     col = iota((64, 512), 1)
     row64 = iota((64, 1), 0)
-    row256 = iota((ROWS, 1), 0)
-    low16 = lanes_low((16, 128))
     keys = [jnp.concatenate([k3[i, hh] for i in range(2 * N3)], axis=0) for hh in range(GH)]
     scores = [dot_t(q2s[hh].reshape(64, 128), keys[hh]) for hh in range(GH)]
     soft = [
@@ -376,35 +389,27 @@
         merge(n2[hh], t2[hh], num3[hh], jnp.where(((row64 >> 2) & 3) == digits[hh][2], soft[hh][1], LOW))
         for hh in range(GH)
     ]
-    both = [
-        merge(
-            n1[hh], t1[hh], spread(both[hh][0], 16),
-            jnp.where(((row256 >> 4) & 3) == digits[hh][1], spread(both[hh][1], 16), LOW),
-        )
-        for hh in range(GH)
-    ]
-    for hh in range(GH):
-        c1 = digits[hh][0]
-        num1, top1 = both[hh]
-        b0, b1, _, _ = bits(sm[x, hh], (64, 128))
+    for hh in range(GH):
+        _, _, b2, b3 = bits(sm[x, hh], (16, 128))
         part = jnp.concatenate(
-            [pick([n0[hh, j, i * 64 : (i + 1) * 64, :] for i in range(4)], b0, b1) for j in range(NX)], axis=0
-        )
-        b0, b1, _, _ = bits(sm[x, hh], (64, 1))
+            [pick([nm[hh, j * 64 + i * 16 : j * 64 + (i + 1) * 16, :] for i in range(4)], b2, b3) for j in range(NX)],
+            axis=0,
+        )
+        _, _, b2, b3 = bits(sm[x, hh], (16, 1))
         part_top = jnp.concatenate(
-            [pick([t0[hh, j, i * 64 : (i + 1) * 64, :] for i in range(4)], b0, b1) for j in range(NX)], axis=0
-        )
-        num, _ = merge(part, part_top, num1, top1)
+            [pick([tm[hh, j * 64 + i * 16 : j * 64 + (i + 1) * 16, :] for i in range(4)], b2, b3) for j in range(NX)],
+            axis=0,
+        )
+        num, _ = merge(part, part_top, *both[hh])
         value = quotient(num, hh % 2 == 0).astype(BF)
-        place = jnp.zeros((16, 128), jnp.int32) + c1
+        place = jnp.zeros((16, 128), jnp.int32) + (digits[hh][0] * 4 + digits[hh][1])
         side = [low16, jnp.logical_not(low16), low16][hh]
-        masks = [(place == i) & side for i in range(4)]
         lanes = slice(hh // 2 * 128, (hh // 2 + 1) * 128)
-        for j in range(NX):
-            for i in range(16):
-                new = value[j * 64 + i % 4 * 16 : j * 64 + i % 4 * 16 + 16]
-                rows = slice(i * 16, (i + 1) * 16)
-                outp[j, rows, lanes] = jnp.where(masks[i // 4], new, outp[j, rows, lanes])
+        for i in range(16):
+            mask = (place == i) & side
+            rows = slice(i * 16, (i + 1) * 16)
+            for j in range(NX):
+                outp[j, rows, lanes] = jnp.where(mask, value[j * 16 : (j + 1) * 16], outp[j, rows, lanes])
     for j in range(NX):
         final = lax.dot_general(
             outp[j], perm[...], (((0,), (0,)), ((), ())), preferred_element_type=F32
@@ -447,6 +452,8 @@
             pltpu.VMEM((GH, NX, ROWS, 1), F32),
             pltpu.VMEM((GH, ROWS, 128), F32),
             pltpu.VMEM((GH, ROWS, 1), F32),
+            pltpu.VMEM((GH, ROWS, 128), F32),
+            pltpu.VMEM((GH, ROWS, 1), F32),
             pltpu.VMEM((GH, 64, 512), F32),
             pltpu.VMEM((GH, 512, 128), BF),
             pltpu.VMEM((GH, 64, 128), F32),

time: 24.9 us -> 23.9 us (0.960)
  Pallas kernels: 24 us -> 23 us
    pallas_call x1, Pallas kernels: 24 us -> 23 us  [per_device(): pl.pallas_call(kernel, out_shape=jax.ShapeDtypeStruct((GH * HD, NX * ROWS...]
where the time goes in v4:
time: 23.9 us; the launch traced here: 23.8 us
  Pallas kernels  23 us (96%)
  local copies, waits for them, and re-layouts  0.75 us (3%)
    pallas_call x1, Pallas kernels, per_device(): pl.pallas_call(kernel, out_shape=jax.ShapeDtypeStruct((GH * HD, NX * ROWS...  23 us
    unnamed x1, local copies, waits for them, and re-layouts  0.75 us

profile of v4, /device:TPU:1, one launch (start us, length us, event | category | flops | bytes accessed | tf_op | source)
XLA Modules:
  0.0 23.8 jit_solution(6470821789415572998)
XLA Ops:
  0.0 23.0 %shard_map.28 = bf16[192,1024]{1,0:T(8,128)(2,1)S(1)} custom-call(bf16[3,256,768]{2,1,0:T(8,128)(2,1)} %qkv.1, s32[3]{0:T(128)} %offs.1), custom_call_target="tpu_custom_call" | custom-call | flops 1000000000 | bytes 2000000 | tf_op jit(solution)/shard_map/pallas_call | solution.py:430
  23.0 0.7 %copy.4 = bf16[1024,192]{0,1:T(8,128)(2,1)} copy(bf16[1024,192]{0,1:T(8,128)(2,1)S(1)} %bitcast.1) | data formatting | bytes 786432

commit v5 on v4

--- a/solution.py
+++ b/solution.py
@@ -261,11 +261,6 @@
     own_s.wait()
     for copy in s_copies:
         copy.wait_recv()
-    e_row, e_col = iota((16, 64), 0), iota((16, 64), 1)
-    for hh in range(GH):
-        chosen = jnp.where(e_col == ((e_row & 12) << 2) + digits[hh][2] * 4 + (e_row & 3), 1.0, 0.0).astype(BF)
-        k3own[hh] = dot(chosen, kv[hh, :, 0:16, :].reshape(64, 128)).astype(BF)
-
     @pl.when(n_later > 0)
     def _():
         pl.semaphore_wait(ready, n_later)
@@ -274,6 +269,10 @@
         send(kv.at[:, :, pl.ds(0, 16), :], k2.at[i], l2_send.at[i], l2_recv.at[i], along_seq(step))
         for i, step in enumerate(L2_STEPS)
     ]
+    e_row, e_col = iota((16, 64), 0), iota((16, 64), 1)
+    for hh in range(GH):
+        chosen = jnp.where(e_col == ((e_row & 12) << 2) + digits[hh][2] * 4 + (e_row & 3), 1.0, 0.0).astype(BF)
+        k3own[hh] = dot(chosen, kv[hh, :, 0:16, :].reshape(64, 128)).astype(BF)
     l3_copies = [
         send(k3own, k3.at[i], l3_send.at[i], l3_recv.at[i], along_seq(step)) for i, step in enumerate(L3_STEPS)
     ]

time: 23.9 us -> 23.8 us (level)
  no operation moved by 1% of the time
where the time goes in v5:
time: 23.8 us; the launch traced here: 23.6 us
  Pallas kernels  22.9 us (96%)
  local copies, waits for them, and re-layouts  0.75 us (3%)
    pallas_call x1, Pallas kernels, per_device(): pl.pallas_call(kernel, out_shape=jax.ShapeDtypeStruct((GH * HD, NX * ROWS...  22.9 us
    unnamed x1, local copies, waits for them, and re-layouts  0.75 us

profile of v5, /device:TPU:1, one launch (start us, length us, event | category | flops | bytes accessed | tf_op | source)
XLA Modules:
  0.0 23.6 jit_solution(15918461598250807909)
XLA Ops:
  0.0 22.9 %shard_map.28 = bf16[192,1024]{1,0:T(8,128)(2,1)S(1)} custom-call(bf16[3,256,768]{2,1,0:T(8,128)(2,1)} %qkv.1, s32[3]{0:T(128)} %offs.1), custom_call_target="tpu_custom_call" | custom-call | flops 1000000000 | bytes 2000000 | tf_op jit(solution)/shard_map/pallas_call | solution.py:429
  22.9 0.7 %copy.4 = bf16[1024,192]{0,1:T(8,128)(2,1)} copy(bf16[1024,192]{0,1:T(8,128)(2,1)S(1)} %bitcast.1) | data formatting | bytes 786432

commit v6 on v5

--- a/solution.py
+++ b/solution.py
@@ -315,10 +315,10 @@
             copy.wait_recv()
         keys = [kv[hh, 2 * seg : 2 * seg + 2].reshape(512, 128) for seg in range(2)]
         values = [ones_and_values(keys[seg]) for seg in range(2)]
-        for pair in ((0, 2), (1, 3)):
+        for pair in ((0, 1, 2, 3),):
             scores = [dot_t(qz[hh, j], keys[j // 2]) for j in pair]
-            soft = [soften(scores[i]) for i in range(2)]
-            nums = [dot(soft[i][0], values[pair[i] // 2]) for i in range(2)]
+            soft = [soften(scores[i]) for i in range(4)]
+            nums = [dot(soft[i][0], values[pair[i] // 2]) for i in range(4)]
             for i, j in enumerate(pair):
                 n0[hh, j] = nums[i]
                 t0[hh, j] = soft[i][1]

time: 23.8 us -> 23.7 us (level)
  no operation moved by 1% of the time
where the time goes in v6:
time: 23.7 us; the launch traced here: 23.6 us
  Pallas kernels  22.9 us (97%)
  local copies, waits for them, and re-layouts  0.75 us (3%)
    pallas_call x1, Pallas kernels, per_device(): pl.pallas_call(kernel, out_shape=jax.ShapeDtypeStruct((GH * HD, NX * ROWS...  22.9 us
    unnamed x1, local copies, waits for them, and re-layouts  0.75 us

profile of v6, /device:TPU:1, one launch (start us, length us, event | category | flops | bytes accessed | tf_op | source)
XLA Modules:
  0.0 23.6 jit_solution(9352156622852559501)
XLA Ops:
  0.0 22.9 %shard_map.28 = bf16[192,1024]{1,0:T(8,128)(2,1)S(1)} custom-call(bf16[3,256,768]{2,1,0:T(8,128)(2,1)} %qkv.1, s32[3]{0:T(128)} %offs.1), custom_call_target="tpu_custom_call" | custom-call | flops 1000000000 | bytes 2000000 | tf_op jit(solution)/shard_map/pallas_call | solution.py:429
  22.9 0.7 %copy.4 = bf16[1024,192]{0,1:T(8,128)(2,1)} copy(bf16[1024,192]{0,1:T(8,128)(2,1)S(1)} %bitcast.1) | data formatting | bytes 786432

commit v7 on v5

--- a/solution.py
+++ b/solution.py
@@ -182,12 +182,6 @@
         ]
 
     q_copies = [send_q(0), send_q(1)]
-    for step in L2_STEPS + L3_STEPS:
-
-        @pl.when(jnp.logical_not(later(step)))
-        def _():
-            pl.semaphore_signal(ready, inc=1, device_id=along_seq(step), device_id_type=MESH)
-
     own_q = pltpu.make_async_copy(qs.at[x], qr.at[:, x], own_sem.at[0])
     own_q.start()
 
@@ -230,6 +224,12 @@
         o_copies[0][3 - k].wait_recv()
         pick_first(lax.rem(x + k, NX))
         s_copies.append(send_rows_to(k, 0, 16, s_send, s_recv))
+    for step in L2_STEPS + L3_STEPS:
+
+        @pl.when(jnp.logical_not(later(step)))
+        def _():
+            pl.semaphore_signal(ready, inc=1, device_id=along_seq(step), device_id_type=MESH)
+
     for g in range(NX):
         for hh in range(GH):
             b0, b1, b2, b3 = bits(sm[g, hh], (16, 128))
@@ -311,6 +311,16 @@
     own_r.wait()
     low16 = lanes_low((16, 128))
     for hh in range(GH):
+        if hh == 2:
+            done = [copy for copy in sends if all(copy is not late for late in (*r_copies[2], f2_copy, f3_copy))]
+            for copy in done:
+                copy.wait_send()
+
+            @pl.when(core == 1)
+            def _():
+                for copy in o_copies[0] + o_copies[1]:
+                    copy.wait_send()
+
         for copy in r_copies[hh]:
             copy.wait_recv()
         keys = [kv[hh, 2 * seg : 2 * seg + 2].reshape(512, 128) for seg in range(2)]
@@ -415,13 +425,8 @@
         )
         out[:, j * ROWS : (j + 1) * ROWS] = final[: GH * HD].astype(BF)
 
-    for copy in sends:
+    for copy in (*r_copies[2], f2_copy, f3_copy):
         copy.wait_send()
-
-    @pl.when(core == 1)
-    def _():
-        for copy in o_copies[0] + o_copies[1]:
-            copy.wait_send()
 
 
 def per_device(qkv, offsets):

time: 23.8 us -> 23.8 us (level)
  no operation moved by 1% of the time
where the time goes in v7:
time: 23.8 us; the launch traced here: 23.7 us
  Pallas kernels  22.9 us (96%)
  local copies, waits for them, and re-layouts  0.75 us (3%)
    pallas_call x1, Pallas kernels, per_device(): pl.pallas_call(kernel, out_shape=jax.ShapeDtypeStruct((GH * HD, NX * ROWS...  22.9 us
    unnamed x1, local copies, waits for them, and re-layouts  0.75 us

profile of v7, /device:TPU:1, one launch (start us, length us, event | category | flops | bytes accessed | tf_op | source)
XLA Modules:
  0.0 23.7 jit_solution(1673216708853597672)
XLA Ops:
  0.0 22.9 %shard_map.28 = bf16[192,1024]{1,0:T(8,128)(2,1)S(1)} custom-call(bf16[3,256,768]{2,1,0:T(8,128)(2,1)} %qkv.1, s32[3]{0:T(128)} %offs.1), custom_call_target="tpu_custom_call" | custom-call | flops 1000000000 | bytes 2000000 | tf_op jit(solution)/shard_map/pallas_call | solution.py:434
  22.9 0.7 %copy.4 = bf16[1024,192]{0,1:T(8,128)(2,1)} copy(bf16[1024,192]{0,1:T(8,128)(2,1)S(1)} %bitcast.1) | data formatting | bytes 786432
